TPU v7x, 128 devices: a whole 4x4x4 slice. The times are simulated.
128 devices in a mesh: axial: 32 (over y, z, core), azim: 4 (over x).
Axes of the slice: x: 4, y: 4, z: 4, core: 2. Of those that a mesh axis runs over, the one named last changes fastest.
Arguments:
- residual: float32 [512, 384, 256], P('axial', 'azim'), may hold values from -6 to 6
- element_scale: float32 [3, 64, 48, 32], P(None, 'axial', 'azim'), may hold values from 0.5 to 2
- basis_fine: float32 [8, 8], replicated, may hold values from -2 to 2
- eigen_fine: float32 [8], replicated, may hold values from 0.5 to 4
- operator_fine: float32 [8, 8], replicated, may hold values from -2 to 2
- basis_mid: float32 [4, 4], replicated, may hold values from -3 to 3
- eigen_mid: float32 [4], replicated, may hold values from 0.5 to 4
- operator_mid: float32 [4, 4], replicated, may hold values from -3 to 3
- basis_low: float32 [2, 2], replicated, may hold values from -4 to 4
- eigen_low: float32 [2], replicated, may hold values from 0.5 to 4
- prolong_mid: float32 [8, 4], replicated, may hold values from -3 to 3
- prolong_low: float32 [4, 2], replicated, may hold values from -4 to 4
- vertex_route: int32 [32, 4, 768, 1], P('axial', 'azim'), may hold values from 0 to 63; in each aligned block of 768 rows (0 to 767, 768 to 1535, ..., all dimensions but the last counted through in order) at most 24 rows name the same one
- coarse_inverse: float32 [32, 4, 1536, 3072], P('axial', 'azim'), may hold values from -2 to 3
Outputs:
- correction: float32 [512, 384, 256], P('axial', 'azim')
Inputs may be any that keep to these rules, and one draw needn't show every extreme that they name: `vertex_route`: among one device's 768 elements no coarse block is named more than 24 times, and one is named exactly 24 times.
All inputs are finite; a program needn't handle non-finite values.
Results may differ from a plain program's by a relative error of at most 0.0003.
Values sent between devices are 32-bit elements; how exact they have to be, the bound alone decides.
A program may use at most 192 MiB of HBM per device.

v0:
```python
import functools

import jax
import jax.numpy as jnp
from jax import lax
from jax.experimental import pallas as pl
from jax.experimental.pallas import tpu as pltpu
from jax.sharding import PartitionSpec as P

F32 = jnp.float32
BF = jnp.bfloat16
HIGHEST = lax.Precision.HIGHEST
MESH = pl.DeviceIdType.MESH

EZ, ER = 12, 32
HALF_CAP = 12
DIRS = ((1, 0), (-1, 0), (0, 1), (0, -1), (1, 1), (1, -1), (-1, 1), (-1, -1))


def iota(shape, dim):
    return lax.broadcasted_iota(jnp.int32, shape, dim)


def split(x):
    high = x.astype(BF)
    return high, (x - high.astype(F32)).astype(BF)


def mm(a, b):
    return jnp.dot(a, b, preferred_element_type=F32)


def mm_right(x, table):
    high, low = split(x)
    return mm(high, table[0]) + mm(high, table[1]) + mm(low, table[0])


def mm_left(table, x):
    high, low = split(x)
    return mm(table[0], high) + mm(table[1], high) + mm(table[0], low)


def stacked_right(x, table):
    high, low = split(x)
    return mm(jnp.concatenate([high, high, low], 1), table)


def stacked_left(table, x):
    high, low = split(x)
    return mm(table, jnp.concatenate([high, high, low], 0))


def picked(condition):
    return jnp.where(condition, 1.0, 0.0).astype(F32)


def quotient(x, size, count):
    if size & (size - 1) == 0:
        return x >> (size.bit_length() - 1)
    total = jnp.zeros_like(x)
    for k in range(1, count):
        total = total + jnp.where(x >= size * k, 1, 0)
    return total


def tables_of(ref):
    m, n = ref.shape
    row, lane = iota((8, 128), 0), iota((8, 128), 1)
    plain = jnp.where(lane < 8, row * 8 + lane, -1)
    turned = jnp.where(lane < 8, lane * 8 + row, -1)
    table = jnp.zeros((8, 128), F32)
    transposed = jnp.zeros((8, 128), F32)
    for i in range(m):
        for j in range(n):
            value = ref[i, j]
            table = jnp.where(plain == i * 8 + j, value, table)
            transposed = jnp.where(turned == i * 8 + j, value, transposed)
    return table, transposed


def spread_columns(table, count, length, place):
    index = place(iota((8, length), 1))
    result = jnp.zeros((8, length), F32)
    for j in range(count):
        result = jnp.where(index == j, table[:, j : j + 1], result)
    return result


def spread_rows(table, length, place):
    high = table.astype(BF).astype(F32)
    rest = table - high
    middle = rest.astype(BF).astype(F32)
    pieces = jnp.concatenate([high, middle, rest - middle], 0).astype(BF)
    index = place(iota((length, 24), 0))
    return mm(picked((iota((length, 24), 1) & 7) == index).astype(BF), pieces)


def left_table(table, m, n, group, joined=False, weighted=False, weigh_input=False):
    rows, columns = m * group * m, n * group * n

    def parts(x, nodes):
        outer = quotient(x, group * nodes, nodes)
        inner = x - outer * (group * nodes)
        block = quotient(inner, nodes, group)
        return outer, block, inner - block * nodes

    first = spread_columns(table, n, columns, lambda x: parts(x, n)[0])
    second = spread_columns(table, n, columns, lambda x: parts(x, n)[2])
    outer = spread_rows(first, rows, lambda x: parts(x, m)[0])
    inner = spread_rows(second, rows, lambda x: parts(x, m)[2])
    shape = (rows, columns)
    _, row_block, q = parts(iota(shape, 0), m)
    _, column_block, j = parts(iota(shape, 1), n)
    value = jnp.where(row_block == column_block, inner, 0.0)
    if joined:
        value = value + jnp.where(
            (q == m - 1) & (row_block + 1 == column_block), second[0:1], 0.0
        )
        value = value + jnp.where(
            (q == 0) & (row_block - 1 == column_block), second[m - 1 : m], 0.0
        )
    if weighted:
        value = jnp.where((q == 0) | (q == m - 1), 0.5 * value, value)
    if weigh_input:
        value = jnp.where((j == 0) | (j == n - 1), 0.5 * value, value)
    return outer * value


def right_table(turned, m, n, joined=False, weighted=False, weigh_input=False):
    rows, columns = ER * n, ER * m
    spread = spread_columns(turned, m, columns, lambda x: x & (m - 1))
    inner = spread_rows(spread, rows, lambda x: x & (n - 1))
    shape = (rows, columns)
    row, column = iota(shape, 0), iota(shape, 1)
    row_block, k = quotient(row, n, ER), row & (n - 1)
    column_block, s = quotient(column, m, ER), column & (m - 1)
    value = jnp.where(row_block == column_block, inner, 0.0)
    if joined:
        value = value + jnp.where(
            (s == m - 1) & (column_block + 1 == row_block), inner[:, 0:1], 0.0
        )
        value = value + jnp.where(
            (s == 0) & (column_block - 1 == row_block), inner[:, m - 1 : m], 0.0
        )
    if weighted:
        shared = ((s == 0) & (column_block > 0)) | ((s == m - 1) & (column_block < ER - 1))
        value = jnp.where(shared, 0.5 * value, value)
    if weigh_input:
        shared = ((k == 0) & (row_block > 0)) | ((k == n - 1) & (row_block < ER - 1))
        value = jnp.where(shared, 0.5 * value, value)
    return value


def put_pair(ref, index, value):
    high, low = split(value)
    ref[index, 0] = high
    ref[index, 1] = low


def put_right(ref, index, value):
    size = value.shape[0]
    high, low = split(value)
    ref[index, 0:size] = high
    ref[index, size : 2 * size] = low
    ref[index, 2 * size : 3 * size] = high


def put_left(ref, index, value):
    size = value.shape[1]
    high, low = split(value)
    ref[index, :, 0:size] = high
    ref[index, :, size : 2 * size] = low
    ref[index, :, 2 * size : 3 * size] = high


def put_scales(scale_ref, eig_ref, n, scale_out, inverse_out):
    rows, lanes = EZ * n, ER * n
    spread_z = picked(quotient(iota((rows, EZ), 0), n, EZ) == iota((rows, EZ), 1))
    spread_r = picked(iota((ER, lanes), 0) == quotient(iota((ER, lanes), 1), n, ER))
    row = iota((rows, lanes), 0) & (n - 1)
    lane = iota((rows, lanes), 1) & (n - 1)
    eig_row = jnp.zeros((rows, lanes), F32)
    eig_lane = jnp.zeros((rows, lanes), F32)
    for k in range(n):
        eig_row = jnp.where(row == k, eig_ref[k], eig_row)
        eig_lane = jnp.where(lane == k, eig_ref[k], eig_lane)
    for a in range(2):
        h = []
        for d in range(3):
            wide = jnp.dot(
                scale_ref[d, a], spread_r, precision=HIGHEST, preferred_element_type=F32
            )
            h.append(
                jnp.dot(spread_z, wide, precision=HIGHEST, preferred_element_type=F32)
            )
        flat = h[1] * eig_row + h[2] * eig_lane
        for i in range(n):
            total = h[0] * eig_ref[i] + flat
            if scale_out is not None:
                scale_out[a * n + i] = total
            inverse_out[a * n + i] = 1.0 / total


def kernel(
    res_hbm, scale_ref, route_ref, inverse_hbm,
    bf_ref, ef_ref, qf_ref, bm_ref, em_ref, qm_ref, bl_ref, el_ref, pm_ref, plow_ref,
    out_ref,
    res, first, work, scale_f, inv_f, rhs_m, smooth_m, work_m, scale_m, inv_m,
    rhs_l, smooth_l, inv_l, total_l,
    right_f, left_f, right_rf, left_rf, right_pf, left_pf,
    right_m, left_m, right_rm, left_rm, right_l, left_l, right_pp, left_pp,
    dense, target_hot, slot_hot, row_hot, place_hot, sel_hot, vector, partial,
    flat_a, send_a, recv_a, flat_b, send_b, recv_b, cs_plane, cs_row, cr_plane, cr_row,
    fs_ax, fr_ax, fs_az, fr_az, fs_dg, fr_dg,
    ms_ax, mr_ax, ms_az, mr_az, ms_dg, mr_dg,
    ls_ax, lr_ax, ls_az, lr_az, ls_dg, lr_dg,
    send_sem, recv_sem, load_sem, all_sem,
    *, n_axial, n_azim,
):
    devices = n_axial * n_azim
    me_a, me_z = lax.axis_index("axial"), lax.axis_index("azim")
    me = me_a * n_azim + me_z

    def device_of(flat):
        return (flat // n_azim, lax.rem(flat, n_azim))

    def neighbour(da, dz):
        return (lax.rem(me_a + n_axial + da, n_axial), lax.rem(me_z + n_azim + dz, n_azim))

    load_res = pltpu.make_async_copy(res_hbm, res, load_sem.at[0])
    load_res.start()
    load_dense = pltpu.make_async_copy(inverse_hbm.at[0, 0], dense, load_sem.at[1])
    load_dense.start()

    barrier = pltpu.get_barrier_semaphore()

    def greet(j, carry):
        pl.semaphore_signal(
            barrier, inc=1, device_id=device_of(lax.rem(me + j, devices)), device_id_type=MESH
        )
        return carry

    lax.fori_loop(1, devices, greet, 0)

    first_device, last_device = me_a == 0, me_a == n_axial - 1
    weight_low_end = jnp.where(first_device, 1.0, 0.5).astype(F32)
    weight_high_end = jnp.where(last_device, 1.0, 0.5).astype(F32)

    faces = {
        8: (fs_ax, fr_ax, fs_az, fr_az, fs_dg, fr_dg),
        4: (ms_ax, mr_ax, ms_az, mr_az, ms_dg, mr_dg),
        2: (ls_ax, lr_ax, ls_az, lr_az, ls_dg, lr_dg),
    }
    pending = []

    def copies_of(e, slot, n):
        s_ax, r_ax, s_az, r_az, s_dg, r_dg = faces[n]
        made = []
        for d, (da, dz) in enumerate(DIRS):
            if d < 2:
                source, target = s_ax.at[slot, d], r_ax.at[slot, d]
            elif d < 4:
                source, target = s_az.at[slot, d - 2], r_az.at[slot, d - 2]
            else:
                source, target = s_dg.at[slot, d - 4], r_dg.at[slot, d - 4]
            made.append(
                pltpu.make_async_remote_copy(
                    src_ref=source, dst_ref=target,
                    send_sem=send_sem.at[e, d], recv_sem=recv_sem.at[e, d],
                    device_id=neighbour(da, dz), device_id_type=MESH,
                )
            )
        return made

    def send_faces(e, slot, n, buf, step, weighted):
        planes, rows, _ = buf.shape
        if step is not None:
            for at in range(step, rows, step):
                both = buf[:, at - 1 : at, :] + buf[:, at : at + 1, :]
                buf[:, at - 1 : at, :] = both
                buf[:, at : at + 1, :] = both
        both = buf[n - 1] + buf[n]
        if weighted:
            both = 0.5 * both
        buf[n - 1] = both
        buf[n] = both
        s_ax, _, s_az, _, s_dg, _ = faces[n]
        s_ax[slot, 0] = buf[planes - 1]
        s_ax[slot, 1] = buf[0]
        s_dg[slot, 0] = buf[planes - 1, rows - 1 : rows]
        s_dg[slot, 1] = buf[planes - 1, 0:1]
        s_dg[slot, 2] = buf[0, rows - 1 : rows]
        s_dg[slot, 3] = buf[0, 0:1]
        for i in range(planes):
            s_az[slot, 0, i : i + 1] = buf[i, rows - 1 : rows]
            s_az[slot, 1, i : i + 1] = buf[i, 0:1]
        made = copies_of(e, slot, n)
        for copy in made:
            copy.start()
        pending.extend(made)
        return made

    def join_faces(made, slot, n, buf, weighted):
        planes, rows, _ = buf.shape
        _, r_ax, _, r_az, _, r_dg = faces[n]
        for copy in made:
            copy.wait_recv()
        for i in range(planes):
            buf[i, 0:1] = buf[i, 0:1] + r_az[slot, 0, i : i + 1]
            buf[i, rows - 1 : rows] = buf[i, rows - 1 : rows] + r_az[slot, 1, i : i + 1]
        for end, plane, device, weight in (
            (0, 0, first_device, weight_low_end),
            (1, planes - 1, last_device, weight_high_end),
        ):
            buf[plane] = buf[plane] + jnp.where(device, 0.0, r_ax[slot, end])
            buf[plane, 0:1] = buf[plane, 0:1] + jnp.where(device, 0.0, r_dg[slot, 2 * end])
            buf[plane, rows - 1 : rows] = buf[plane, rows - 1 : rows] + jnp.where(
                device, 0.0, r_dg[slot, 2 * end + 1]
            )
            if weighted:
                buf[plane] = buf[plane] * weight

    def fine_loop(body):
        def step(t, carry):
            a = t // 3
            g = lax.rem(t, 3)
            body(a, g)
            return carry

        lax.fori_loop(0, 6, step, 0)

    def cut(ref, a, g, planes=8, rows=32):
        return ref.at[
            pl.ds(pl.multiple_of(a * planes, planes), planes),
            pl.ds(pl.multiple_of(g * rows, rows), rows),
        ]

    def fine_pass(source, which, factor, result):
        def body(a, g):
            x = source(a, g).reshape(256, 256)
            y = stacked_right(x, right_f[2 * which])
            z = stacked_left(left_f[2 * which], y)
            z = z * cut(factor, a, g)[...].reshape(256, 256)
            u = stacked_right(z, right_f[2 * which + 1])
            w = stacked_left(left_f[2 * which + 1], u)
            cut(result, a, g)[...] = w.reshape(8, 32, 256)

        fine_loop(body)

    basis, basis_t = tables_of(bf_ref)
    put_right(right_f, 0, right_table(basis, 8, 8))
    put_left(left_f, 0, left_table(basis_t, 8, 8, 4))
    put_right(right_f, 1, right_table(basis_t, 8, 8, joined=True, weighted=True))
    put_left(left_f, 1, left_table(basis, 8, 8, 4, joined=True, weighted=True))
    put_scales(scale_ref, ef_ref, 8, scale_f, inv_f)

    load_res.wait()
    fine_pass(lambda a, g: cut(res, a, g)[...], 0, inv_f, first)
    pl.semaphore_wait(barrier, devices - 1)
    made = send_faces(0, 0, 8, first, 32, True)

    oper, oper_t = tables_of(qf_ref)
    put_right(right_f, 2, right_table(oper, 8, 8))
    put_left(left_f, 2, left_table(oper_t, 8, 8, 4))
    put_right(right_f, 3, right_table(oper_t, 8, 8, joined=True))
    put_left(left_f, 3, left_table(oper, 8, 8, 4, joined=True))

    join_faces(made, 0, 8, first, True)
    fine_pass(lambda a, g: cut(first, a, g)[...], 1, scale_f, work)
    made = send_faces(1, 1, 8, work, 32, False)

    put_scales(scale_ref, em_ref, 4, scale_m, inv_m)
    pm, pm_t = tables_of(pm_ref)
    put_right(right_rf, 0, right_table(pm, 4, 8, joined=True, weigh_input=True))
    put_left(left_rf, 0, left_table(pm_t, 4, 8, 4, joined=True, weigh_input=True))
    basis, basis_t = tables_of(bm_ref)
    put_pair(right_m, 0, right_table(basis, 4, 4))
    put_pair(left_m, 0, left_table(basis_t, 4, 4, EZ))
    put_pair(right_m, 1, right_table(basis_t, 4, 4, joined=True, weighted=True))
    put_pair(left_m, 1, left_table(basis, 4, 4, EZ, joined=True, weighted=True))

    join_faces(made, 1, 8, work, False)
    fine_pass(lambda a, g: cut(res, a, g)[...] - cut(work, a, g)[...], 0, inv_f, out_ref)
    made = send_faces(2, 2, 8, out_ref, 32, True)

    oper, oper_t = tables_of(qm_ref)
    put_pair(right_m, 2, right_table(oper, 4, 4))
    put_pair(left_m, 2, left_table(oper_t, 4, 4, EZ))
    put_pair(right_m, 3, right_table(oper_t, 4, 4, joined=True))
    put_pair(left_m, 3, left_table(oper, 4, 4, EZ, joined=True))
    put_scales(scale_ref, el_ref, 2, None, inv_l)

    join_faces(made, 2, 8, out_ref, True)

    def add_up(a, g):
        total = cut(first, a, g)[...] + cut(out_ref, a, g)[...]
        cut(first, a, g)[...] = total
        return total

    fine_pass(add_up, 1, scale_f, work)
    made = send_faces(3, 3, 8, work, 32, False)

    plow, plow_t = tables_of(plow_ref)
    put_pair(right_rm, 0, right_table(plow, 2, 4, joined=True, weigh_input=True))
    put_pair(left_rm, 0, left_table(plow_t, 2, 4, EZ, joined=True, weigh_input=True))
    basis, basis_t = tables_of(bl_ref)
    put_pair(right_l, 0, right_table(basis, 2, 2))
    put_pair(left_l, 0, left_table(basis_t, 2, 2, EZ))
    put_pair(right_l, 1, right_table(basis_t, 2, 2, joined=True, weighted=True))
    put_pair(left_l, 1, left_table(basis, 2, 2, EZ, joined=True, weighted=True))

    join_faces(made, 3, 8, work, False)

    def restrict(a, g):
        x = cut(res, a, g)[...] - cut(work, a, g)[...]
        low = jnp.where(a == 0, weight_low_end, 0.5)
        high = jnp.where(a == 0, 0.5, weight_high_end)
        x = jnp.concatenate([x[0:1] * low, x[1:7], x[7:8] * high], 0)
        y = stacked_right(x.reshape(256, 256), right_rf[0])
        z = stacked_left(left_rf[0], y)
        cut(rhs_m, a, g, 4, 16)[...] = z.reshape(4, 16, 128)

    fine_loop(restrict)
    made = send_faces(4, 0, 4, rhs_m, 16, False)

    route = route_ref[...]
    hot = picked(iota((64, 768), 0) == route)
    target_hot[...] = hot.astype(BF)
    earlier = picked(iota((768, 768), 0) < iota((768, 768), 1)).astype(BF)
    rank = jnp.sum(mm(target_hot[...], earlier) * hot, axis=0, keepdims=True)
    slot_hot[...] = picked(iota((128, 768), 0).astype(F32) == rank)
    half = jnp.where(rank >= HALF_CAP, 1.0, 0.0)
    owner = 2.0 * route.astype(F32) + half
    row_hot[...] = picked(iota((128, 768), 0).astype(F32) == owner).astype(BF)
    place_hot[...] = picked(iota((16, 768), 0).astype(F32) == rank - HALF_CAP * half)

    join_faces(made, 0, 4, rhs_m, False)

    def small_pass(x, n, right, left, which, factor):
        planes, rows, lanes = x.shape
        for side in range(2):
            y = mm_right(x.reshape(planes * rows, lanes), right.at[2 * which + side])
            y = y.reshape(2, n * rows, lanes)
            z = [mm_left(left.at[2 * which + side], y[a]) for a in range(2)]
            x = jnp.concatenate([v.reshape(n, rows, lanes) for v in z], 0)
            if side == 0:
                x = x * factor[...]
        return x

    smooth_m[...] = small_pass(rhs_m[...], 4, right_m, left_m, 0, inv_m)
    made = send_faces(5, 1, 4, smooth_m, None, True)
    put_right(right_pf, 0, right_table(pm_t, 8, 4))
    put_pair(left_pf, 0, left_table(pm, 8, 4, 4))
    join_faces(made, 1, 4, smooth_m, True)

    work_m[...] = small_pass(smooth_m[...], 4, right_m, left_m, 1, scale_m)
    made = send_faces(6, 2, 4, work_m, None, False)
    both = jnp.zeros((8, 128), F32)
    both_t = jnp.zeros((8, 128), F32)
    for k in range(4):
        both = both + pm[:, k : k + 1] * plow[k : k + 1, :]
        both_t = both_t + plow_t[:, k : k + 1] * pm_t[k : k + 1, :]
    put_pair(right_pp, 0, right_table(both_t, 8, 2))
    put_pair(left_pp, 0, left_table(both, 8, 2, 4))
    join_faces(made, 2, 4, work_m, False)

    x = rhs_m[...] - work_m[...]
    x = jnp.concatenate(
        [x[0:1] * weight_low_end, x[1:3], x[3:5] * 0.5, x[5:7], x[7:8] * weight_high_end], 0
    )
    y = mm_right(x.reshape(384, 128), right_rm.at[0]).reshape(2, 192, 64)
    for a in range(2):
        rhs_l[2 * a : 2 * a + 2] = mm_left(left_rm.at[0], y[a]).reshape(2, 24, 64)
    made = send_faces(7, 0, 2, rhs_l, None, False)

    slot = iota((128, 3072), 0)
    lane = iota((1, 3072), 1)
    half_lane = jnp.where(lane >= 1536, 1, 0)
    rest = lane - 1536 * half_lane
    source = jnp.floor((rest.astype(F32) + 0.5) * (1.0 / HALF_CAP)).astype(jnp.int32)
    wanted = half_lane * HALF_CAP + rest - source * HALF_CAP
    sel_hot[...] = picked(slot == wanted).astype(BF)
    join_faces(made, 0, 2, rhs_l, False)

    values = []
    lane = iota((24, 384), 1)
    mine = iota((24, 384), 0) == 2 * (lane >> 5)
    pick_r = picked(iota((64, 384), 0) == 2 * (iota((64, 384), 1) & 31))
    for a in range(2):
        wide = jnp.dot(rhs_l[2 * a], pick_r, precision=HIGHEST, preferred_element_type=F32)
        values.append(jnp.sum(jnp.where(mine, wide, 0.0), axis=0, keepdims=True))
    values = jnp.concatenate(values, 1)
    high, low = split(slot_hot[...] * values)
    nt = (((1,), (1,)), ((), ()))
    flat_a[...] = lax.dot_general(
        target_hot[...], high, nt, preferred_element_type=F32
    ) + lax.dot_general(target_hot[...], low, nt, preferred_element_type=F32)
    for t in range(64):
        send_a[t] = flat_a[t : t + 1]

    def spread_out(source_of, target, sem, row_of):
        def start(j, carry):
            other = lax.rem(me + j, devices)
            pltpu.make_async_remote_copy(
                src_ref=source_of.at[row_of(other)], dst_ref=target.at[me],
                send_sem=all_sem.at[sem], recv_sem=all_sem.at[sem + 1],
                device_id=device_of(other), device_id_type=MESH,
            ).start()
            return carry

        lax.fori_loop(1, devices, start, 0)
        target[me] = source_of[row_of(me)]

    def wait_all(target, sem):
        some = target.at[pl.ds(0, devices - 1)]
        pltpu.make_async_copy(some, some, all_sem.at[sem]).wait()

    spread_out(send_a, recv_a, 0, lambda other: other // 2)

    smooth_l[...] = small_pass(rhs_l[...], 2, right_l, left_l, 0, inv_l)
    made = send_faces(8, 1, 2, smooth_l, None, True)

    def prolong(a, g):
        x = cut(smooth_m, a, g, 4, 16)[...].reshape(64, 128)
        y = stacked_right(x, right_pf[0])
        z = mm_left(left_pf.at[0], y)
        cut(out_ref, a, g)[...] = cut(first, a, g)[...] + z.reshape(8, 32, 256)

    fine_loop(prolong)
    join_faces(made, 1, 2, smooth_l, True)

    wait_all(recv_a, 1)
    for d in range(devices):
        flat_b[d : d + 1] = recv_a[d]
    high, low = split(flat_b[...])
    wide = mm(high, sel_hot[...]) + mm(low, sel_hot[...])
    wide = jnp.where(iota((128, 3072), 0) == source, wide, 0.0)
    vector[...] = jnp.broadcast_to(jnp.sum(wide, axis=0, keepdims=True), (8, 3072))
    load_dense.wait()

    def rows_of(r, carry):
        base = pl.multiple_of(r * 32, 32)
        sums = [None] * 4
        for c in range(24):
            v = vector[:, c * 128 : (c + 1) * 128]
            for k in range(4):
                term = dense[pl.ds(base + 8 * k, 8), c * 128 : (c + 1) * 128] * v
                sums[k] = term if sums[k] is None else sums[k] + term
        for k in range(4):
            partial[pl.ds(base + 8 * k, 8), :] = sums[k]
        return carry

    lax.fori_loop(0, 48, rows_of, 0)
    high, low = split(partial[...])
    ones = jnp.ones((128, 128), BF)
    sums = mm(high, ones) + mm(low, ones)
    row = iota((1536, 128), 0)
    group = jnp.floor((row.astype(F32) + 0.5) * (1.0 / HALF_CAP)).astype(jnp.int32)
    sums = jnp.where(iota((1536, 128), 1) == row - group * HALF_CAP, sums, 0.0)
    high, low = split(sums)
    lane = iota((1, 1536), 1)
    group = jnp.floor((lane.astype(F32) + 0.5) * (1.0 / HALF_CAP)).astype(jnp.int32)
    gather = picked(iota((128, 1536), 0) == group).astype(BF)
    flat_b[...] = mm(gather, high) + mm(gather, low)
    for d in range(devices):
        send_b[d] = flat_b[d : d + 1]
    spread_out(send_b, recv_b, 2, lambda other: other)
    wait_all(recv_b, 3)
    for d in range(devices):
        flat_b[d : d + 1] = recv_b[d]

    turned = jnp.transpose(flat_b[...])[0:16]
    high, low = split(turned)
    answers = mm(high, row_hot[...]) + mm(low, row_hot[...])
    answers = jnp.sum(answers * place_hot[...], axis=0, keepdims=True)
    row = iota((24, 384), 0)
    belongs = (iota((24, 384), 1) >> 5) == ((row + 1) >> 1)
    to_lanes = picked(
        (iota((384, 64), 0) & 31) == ((iota((384, 64), 1) + 1) >> 1)
    ).astype(BF)
    grids = []
    for a in range(2):
        high, low = split(jnp.where(belongs, answers[:, a * 384 : (a + 1) * 384], 0.0))
        grids.append(mm(high, to_lanes) + mm(low, to_lanes))
    cs_plane[...] = grids[0]
    cs_row[0] = grids[0][0:1]
    cs_row[1] = grids[1][0:1]
    made = []
    for k, (source, target, da, dz) in enumerate((
        (cs_plane, cr_plane, -1, 0),
        (cs_row, cr_row.at[pl.ds(0, 2)], 0, -1),
        (cs_row.at[0], cr_row.at[2], -1, -1),
    )):
        copy = pltpu.make_async_remote_copy(
            src_ref=source, dst_ref=target,
            send_sem=send_sem.at[9, k], recv_sem=recv_sem.at[9, k],
            device_id=neighbour(da, dz), device_id_type=MESH,
        )
        copy.start()
        made.append(copy)
    pending.extend(made)
    for copy in made:
        copy.wait_recv()
    last_row = iota((24, 64), 0) == 23
    lower = jnp.where(last_row, cr_row[0], grids[0])
    upper = jnp.where(last_row, cr_row[1], grids[1])
    beyond = jnp.where(last_device, 0.0, jnp.where(last_row, cr_row[2], cr_plane[...]))
    total_l[0] = smooth_l[0] + lower
    total_l[1] = smooth_l[1] + upper
    total_l[2] = smooth_l[2] + upper
    total_l[3] = smooth_l[3] + beyond

    wide = mm_right(total_l[...].reshape(96, 64), right_pp.at[0]).reshape(4, 24, 256)
    for a in range(2):
        for g in range(3):
            x = wide[2 * a : 2 * a + 2, 8 * g : 8 * g + 8].reshape(16, 256)
            z = mm_left(left_pp.at[0], x).reshape(8, 32, 256)
            out_ref[8 * a : 8 * a + 8, 32 * g : 32 * g + 32] += z

    for copy in pending:
        copy.wait_send()
    wait_all(recv_a, 0)
    wait_all(recv_b, 2)


def on_device(
    residual, element_scale, basis_fine, eigen_fine, operator_fine, basis_mid, eigen_mid,
    operator_mid, basis_low, eigen_low, prolong_mid, prolong_low, vertex_route, coarse_inverse,
):
    devices = lax.axis_size("axial") * lax.axis_size("azim")

    def vm(*shape, dtype=F32):
        return pltpu.VMEM(shape, dtype)

    def face_buffers(count, planes, rows, lanes):
        return [
            vm(count, 2, rows, lanes), vm(count, 2, rows, lanes),
            vm(count, 2, planes, lanes), vm(count, 2, planes, lanes),
            vm(count, 4, 1, lanes), vm(count, 4, 1, lanes),
        ]

    fine, mid, low = (16, 96, 256), (8, 48, 128), (4, 24, 64)
    scratch = [
        vm(*fine), vm(*fine), vm(*fine), vm(*fine), vm(*fine),
        vm(*mid), vm(*mid), vm(*mid), vm(*mid), vm(*mid),
        vm(*low), vm(*low), vm(*low), vm(*low),
        vm(4, 768, 256, dtype=BF), vm(4, 256, 768, dtype=BF),
        vm(1, 768, 128, dtype=BF), vm(1, 64, 768, dtype=BF),
        vm(1, 384, 256, dtype=BF), vm(1, 2, 256, 64, dtype=BF),
        vm(4, 2, 128, 128, dtype=BF), vm(4, 2, 192, 192, dtype=BF),
        vm(1, 2, 128, 64, dtype=BF), vm(1, 2, 48, 192, dtype=BF),
        vm(2, 2, 64, 64, dtype=BF), vm(2, 2, 48, 48, dtype=BF),
        vm(1, 2, 64, 256, dtype=BF), vm(1, 2, 256, 16, dtype=BF),
        vm(1536, 3072), vm(64, 768, dtype=BF), vm(128, 768), vm(128, 768, dtype=BF),
        vm(16, 768), vm(128, 3072, dtype=BF), vm(8, 3072), vm(1536, 128),
        vm(64, 128), vm(64, 1, 128), vm(devices, 1, 128),
        vm(devices, 128), vm(devices, 1, 128), vm(devices, 1, 128),
        vm(24, 64), vm(2, 1, 64), vm(24, 64), vm(3, 1, 64),
        *face_buffers(4, *fine), *face_buffers(3, *mid), *face_buffers(2, *low),
        pltpu.SemaphoreType.DMA((10, 8)), pltpu.SemaphoreType.DMA((10, 8)),
        pltpu.SemaphoreType.DMA((2,)), pltpu.SemaphoreType.DMA((4,)),
    ]
    in_vmem = pl.BlockSpec(memory_space=pltpu.VMEM)
    in_smem = pl.BlockSpec(memory_space=pltpu.SMEM)
    anywhere = pl.BlockSpec(memory_space=pl.ANY)
    call = pl.pallas_call(
        functools.partial(
            kernel, n_axial=lax.axis_size("axial"), n_azim=lax.axis_size("azim")
        ),
        out_shape=jax.ShapeDtypeStruct(residual.shape, F32),
        in_specs=[anywhere, in_vmem, in_vmem, anywhere] + [in_smem] * 10,
        out_specs=in_vmem,
        scratch_shapes=scratch,
        compiler_params=pltpu.CompilerParams(
            collective_id=0, has_side_effects=True, vmem_limit_bytes=58 * 1024 * 1024
        ),
        cost_estimate=pl.CostEstimate(
            flops=12_000_000_000, bytes_accessed=24_000_000, transcendentals=0
        ),
    )
    return call(
        residual, element_scale, vertex_route.reshape(1, -1), coarse_inverse,
        basis_fine, eigen_fine, operator_fine, basis_mid, eigen_mid, operator_mid,
        basis_low, eigen_low, prolong_mid, prolong_low,
    )


def solution(mesh):
    return jax.shard_map(
        on_device,
        mesh=mesh,
        in_specs=(
            P("axial", "azim", None),
            P(None, "axial", "azim", None),
            P(), P(), P(), P(), P(), P(), P(), P(), P(), P(),
            P("axial", "azim", None, None),
            P("axial", "azim", None, None),
        ),
        out_specs=P("axial", "azim", None),
        check_vma=False,
    )
```

profile of v0, /device:TPU:1, one launch (start us, length us, event | category | flops | bytes accessed | tf_op | source)
XLA Modules:
  0.0 117.5 jit_solution(1417845496644593879)
XLA Ops:
  0.0 1.3 %copy.17.plow_ref = f32[4,2]{1,0:T(4,128)} copy(f32[4,2]{0,1:T(2,128)} %param.25) | data formatting | bytes 64 | tf_op args[11]
  1.3 1.3 %copy.16.pm_ref = f32[8,4]{1,0:T(8,128)} copy(f32[8,4]{0,1:T(4,128)} %param.24) | data formatting | bytes 256 | tf_op args[10]
  2.7 1.4 %copy.15.scale_ref = f32[3,2,12,32]{3,2,1,0:T(8,128)} copy(f32[3,2,12,32]{3,1,2,0:T(2,128)} %param.15) | data formatting | bytes 18432 | tf_op args[1]
  4.1 110.7 %shard_map.136 = f32[16,96,256]{2,1,0:T(8,128)} custom-call(f32[16,96,256]{2,1,0:T(8,128)} %res_hbm.1, f32[3,2,12,32]{3,2,1,0:T(8,128)} %copy.15.scale_ref, s32[1,768]{1,0:T(1,128)} %bitcast.1, f32[1,1,1536,3072]{3,2,1,0:T(8,128)} %inverse_hbm.1, f32[8,8]{1,0:T(8,128)} %bf_ref.1, f32[8]{0:T(128)} %ef_ref.1, f32[8,8]{1,0:T(8,128)} %qf_ref.1, f32[4,4]{1,0:T(4,128)} %bm_ref.1, ...), custom_call_target="tpu_custom_call" | custom-call | flops 12000000000 | bytes 24000000 | tf_op jit(solution)/shard_map/pallas_call | solution.py:681
  114.8 2.7 %copy.19 = f32[16,96,256]{2,1,0:T(8,128)} copy(f32[16,96,256]{2,1,0:T(8,128)} %shard_map.136) | data formatting | bytes 3145728
where the time goes:
time: 118 us; the launch traced here: 117 us
  Pallas kernels  111 us (94%)
  local copies, waits for them, and re-layouts  6.76 us (6%)
    pallas_call x1, Pallas kernels, on_device(): call(residual, element_scale, vertex_route.reshape(1, -1), coarse_inverse...  111 us
    unnamed x4, local copies, waits for them, and re-layouts  6.76 us

commit v1 on v0

--- a/solution.py
+++ b/solution.py
@@ -40,14 +40,45 @@
     return mm(table[0], high) + mm(table[1], high) + mm(table[0], low)
 
 
-def stacked_right(x, table):
+def wide_right(x, table):
     high, low = split(x)
-    return mm(jnp.concatenate([high, high, low], 1), table)
-
-
-def stacked_left(table, x):
-    high, low = split(x)
-    return mm(table, jnp.concatenate([high, high, low], 0))
+    both = mm(jnp.concatenate([high, low], 1), table)
+    size = table.shape[1] // 2
+    return both[:, :size] + both[:, size:]
+
+
+def wide_left(table, blocks):
+    high, low = split(jnp.concatenate(blocks, 1))
+    both = mm(table, jnp.concatenate([high, low], 0))
+    size = table.shape[0] // 2
+    both = both[:size] + both[size:]
+    lanes = blocks[0].shape[1]
+    return [both[:, k * lanes : (k + 1) * lanes] for k in range(len(blocks))]
+
+
+def thrice_left(table, blocks):
+    high, low = split(jnp.concatenate(blocks, 1))
+    both = mm(table, jnp.concatenate([high, high, low], 0))
+    lanes = blocks[0].shape[1]
+    return [both[:, k * lanes : (k + 1) * lanes] for k in range(len(blocks))]
+
+
+def cut_rows(x, n, rows):
+    planes, length, lanes = x.shape
+    return [
+        x[a * n : a * n + n, r : r + rows].reshape(n * rows, lanes)
+        for a in range(planes // n)
+        for r in range(0, length, rows)
+    ]
+
+
+def paste_rows(blocks, n):
+    rows, lanes = blocks[0].shape[0] // n, blocks[0].shape[1]
+    half = len(blocks) // 2
+    blocks = [b.reshape(n, rows, lanes) for b in blocks]
+    return jnp.concatenate(
+        [jnp.concatenate(blocks[:half], 1), jnp.concatenate(blocks[half:], 1)], 0
+    )
 
 
 def picked(condition):
@@ -63,8 +94,8 @@
     return total
 
 
-def tables_of(ref):
-    m, n = ref.shape
+def tables_of(ref, turned_in=False):
+    n, m = ref.shape if turned_in else ref.shape[::-1]
     row, lane = iota((8, 128), 0), iota((8, 128), 1)
     plain = jnp.where(lane < 8, row * 8 + lane, -1)
     turned = jnp.where(lane < 8, lane * 8 + row, -1)
@@ -72,7 +103,7 @@
     transposed = jnp.zeros((8, 128), F32)
     for i in range(m):
         for j in range(n):
-            value = ref[i, j]
+            value = ref[j, i] if turned_in else ref[i, j]
             table = jnp.where(plain == i * 8 + j, value, table)
             transposed = jnp.where(turned == i * 8 + j, value, transposed)
     return table, transposed
@@ -95,8 +126,11 @@
     return mm(picked((iota((length, 24), 1) & 7) == index).astype(BF), pieces)
 
 
-def left_table(table, m, n, group, joined=False, weighted=False, weigh_input=False):
+def left_table(table, m, n, group, joined=False, weighted=False, weigh_input=False, copies=1):
     rows, columns = m * group * m, n * group * n
+
+    def once(x):
+        return x if copies == 1 else x - columns * quotient(x, columns, copies)
 
     def parts(x, nodes):
         outer = quotient(x, group * nodes, nodes)
@@ -104,13 +138,13 @@
         block = quotient(inner, nodes, group)
         return outer, block, inner - block * nodes
 
-    first = spread_columns(table, n, columns, lambda x: parts(x, n)[0])
-    second = spread_columns(table, n, columns, lambda x: parts(x, n)[2])
+    first = spread_columns(table, n, copies * columns, lambda x: parts(once(x), n)[0])
+    second = spread_columns(table, n, copies * columns, lambda x: parts(once(x), n)[2])
     outer = spread_rows(first, rows, lambda x: parts(x, m)[0])
     inner = spread_rows(second, rows, lambda x: parts(x, m)[2])
-    shape = (rows, columns)
+    shape = (rows, copies * columns)
     _, row_block, q = parts(iota(shape, 0), m)
-    _, column_block, j = parts(iota(shape, 1), n)
+    _, column_block, j = parts(once(iota(shape, 1)), n)
     value = jnp.where(row_block == column_block, inner, 0.0)
     if joined:
         value = value + jnp.where(
@@ -126,14 +160,17 @@
     return outer * value
 
 
-def right_table(turned, m, n, joined=False, weighted=False, weigh_input=False):
-    rows, columns = ER * n, ER * m
-    spread = spread_columns(turned, m, columns, lambda x: x & (m - 1))
+def right_table(
+    turned, m, n, count=ER, joined=False, weighted=False, weigh_input=False,
+    first=True, last=True, copies=1,
+):
+    rows, columns = count * n, count * m
+    spread = spread_columns(turned, m, copies * columns, lambda x: x & (m - 1))
     inner = spread_rows(spread, rows, lambda x: x & (n - 1))
-    shape = (rows, columns)
-    row, column = iota(shape, 0), iota(shape, 1)
-    row_block, k = quotient(row, n, ER), row & (n - 1)
-    column_block, s = quotient(column, m, ER), column & (m - 1)
+    shape = (rows, copies * columns)
+    row, column = iota(shape, 0), iota(shape, 1) & (columns - 1)
+    row_block, k = quotient(row, n, count), row & (n - 1)
+    column_block, s = quotient(column, m, count), column & (m - 1)
     value = jnp.where(row_block == column_block, inner, 0.0)
     if joined:
         value = value + jnp.where(
@@ -142,12 +179,19 @@
         value = value + jnp.where(
             (s == 0) & (column_block - 1 == row_block), inner[:, m - 1 : m], 0.0
         )
+
+    def halved(place, block, nodes, value):
+        low, high = place == 0, place == nodes - 1
+        if first:
+            low = low & (block > 0)
+        if last:
+            high = high & (block < count - 1)
+        return jnp.where(low | high, 0.5 * value, value)
+
     if weighted:
-        shared = ((s == 0) & (column_block > 0)) | ((s == m - 1) & (column_block < ER - 1))
-        value = jnp.where(shared, 0.5 * value, value)
+        value = halved(s, column_block, m, value)
     if weigh_input:
-        shared = ((k == 0) & (row_block > 0)) | ((k == n - 1) & (row_block < ER - 1))
-        value = jnp.where(shared, 0.5 * value, value)
+        value = halved(k, row_block, n, value)
     return value
 
 
@@ -158,19 +202,34 @@
 
 
 def put_right(ref, index, value):
-    size = value.shape[0]
+    rows, columns = value.shape
     high, low = split(value)
-    ref[index, 0:size] = high
-    ref[index, size : 2 * size] = low
-    ref[index, 2 * size : 3 * size] = high
+    for k in range(2):
+        ref[index, k * rows : (k + 1) * rows, 0:columns] = high
+        ref[index, k * rows : (k + 1) * rows, columns : 2 * columns] = low
 
 
 def put_left(ref, index, value):
-    size = value.shape[1]
+    rows, columns = value.shape
     high, low = split(value)
-    ref[index, :, 0:size] = high
-    ref[index, :, size : 2 * size] = low
-    ref[index, :, 2 * size : 3 * size] = high
+    for k in range(2):
+        ref[index, 0:rows, k * columns : (k + 1) * columns] = high
+        ref[index, rows : 2 * rows, k * columns : (k + 1) * columns] = low
+
+
+def put_left_twice(ref, index, value):
+    rows = value.shape[0]
+    high, low = split(value)
+    ref[index, 0:rows] = high
+    ref[index, rows : 2 * rows] = low
+
+
+def put_left_thrice(ref, index, value):
+    columns = value.shape[1] // 3
+    high, low = split(value)
+    lane = iota(value.shape, 1)
+    middle = (lane >= columns) & (lane < 2 * columns)
+    ref[index] = jnp.where(middle, low.astype(F32), high.astype(F32)).astype(BF)
 
 
 def put_scales(scale_ref, eig_ref, n, scale_out, inverse_out):
@@ -188,7 +247,7 @@
         h = []
         for d in range(3):
             wide = jnp.dot(
-                scale_ref[d, a], spread_r, precision=HIGHEST, preferred_element_type=F32
+                scale_ref[d, :, a], spread_r, precision=HIGHEST, preferred_element_type=F32
             )
             h.append(
                 jnp.dot(spread_z, wide, precision=HIGHEST, preferred_element_type=F32)
@@ -205,12 +264,12 @@
     res_hbm, scale_ref, route_ref, inverse_hbm,
     bf_ref, ef_ref, qf_ref, bm_ref, em_ref, qm_ref, bl_ref, el_ref, pm_ref, plow_ref,
     out_ref,
-    res, first, work, scale_f, inv_f, rhs_m, smooth_m, work_m, scale_m, inv_m,
+    res, first, second, work, scale_f, inv_f, rhs_m, smooth_m, work_m, scale_m, inv_m,
     rhs_l, smooth_l, inv_l, total_l,
     right_f, left_f, right_rf, left_rf, right_pf, left_pf,
     right_m, left_m, right_rm, left_rm, right_l, left_l, right_pp, left_pp,
     dense, target_hot, slot_hot, row_hot, place_hot, sel_hot, vector, partial,
-    flat_a, send_a, recv_a, flat_b, send_b, recv_b, cs_plane, cs_row, cr_plane, cr_row,
+    flat_a, send_a, stage_a, recv_a, flat_b, send_b, stage_b, recv_b, cs_plane, cs_row, cr_plane, cr_row,
     fs_ax, fr_ax, fs_az, fr_az, fs_dg, fr_dg,
     ms_ax, mr_ax, ms_az, mr_az, ms_dg, mr_dg,
     ls_ax, lr_ax, ls_az, lr_az, ls_dg, lr_dg,
@@ -219,10 +278,6 @@
 ):
     devices = n_axial * n_azim
     me_a, me_z = lax.axis_index("axial"), lax.axis_index("azim")
-    me = me_a * n_azim + me_z
-
-    def device_of(flat):
-        return (flat // n_azim, lax.rem(flat, n_azim))
 
     def neighbour(da, dz):
         return (lax.rem(me_a + n_axial + da, n_axial), lax.rem(me_z + n_azim + dz, n_azim))
@@ -234,13 +289,25 @@
 
     barrier = pltpu.get_barrier_semaphore()
 
-    def greet(j, carry):
-        pl.semaphore_signal(
-            barrier, inc=1, device_id=device_of(lax.rem(me + j, devices)), device_id_type=MESH
-        )
+    def greet(device):
+        pl.semaphore_signal(barrier, inc=1, device_id=device, device_id_type=MESH)
+
+    def along(j):
+        return (lax.rem(me_a + j, n_axial), me_z)
+
+    def around(j):
+        return (me_a, lax.rem(me_z + j, n_azim))
+
+    def greet_along(j, carry):
+        greet(along(j))
         return carry
 
-    lax.fori_loop(1, devices, greet, 0)
+    for da, dz in DIRS[4:]:
+        greet(neighbour(da, dz))
+    for j in range(1, n_azim):
+        greet(around(j))
+    lax.fori_loop(1, n_axial, greet_along, 0)
+    greeted = 4 + n_azim - 1 + n_axial - 1
 
     first_device, last_device = me_a == 0, me_a == n_axial - 1
     weight_low_end = jnp.where(first_device, 1.0, 0.5).astype(F32)
@@ -320,89 +387,97 @@
             if weighted:
                 buf[plane] = buf[plane] * weight
 
-    def fine_loop(body):
-        def step(t, carry):
-            a = t // 3
-            g = lax.rem(t, 3)
-            body(a, g)
-            return carry
-
-        lax.fori_loop(0, 6, step, 0)
-
-    def cut(ref, a, g, planes=8, rows=32):
-        return ref.at[
-            pl.ds(pl.multiple_of(a * planes, planes), planes),
-            pl.ds(pl.multiple_of(g * rows, rows), rows),
-        ]
-
-    def fine_pass(source, which, factor, result):
-        def body(a, g):
-            x = source(a, g).reshape(256, 256)
-            y = stacked_right(x, right_f[2 * which])
-            z = stacked_left(left_f[2 * which], y)
-            z = z * cut(factor, a, g)[...].reshape(256, 256)
-            u = stacked_right(z, right_f[2 * which + 1])
-            w = stacked_left(left_f[2 * which + 1], u)
-            cut(result, a, g)[...] = w.reshape(8, 32, 256)
-
-        fine_loop(body)
+    def fine_right(x, which, joined):
+        planes, rows, lanes = x.shape
+        x = x.reshape(planes * rows, lanes)
+        left = wide_right(x[:, :128], right_f[2 * which])
+        right = wide_right(x[:, 128:], right_f[2 * which + 1])
+        if joined:
+            lane = iota(left.shape, 1)
+            left, right = (
+                left + jnp.where(lane == 127, pltpu.roll(right, 127, 1), 0.0),
+                right + jnp.where(lane == 0, pltpu.roll(left, 1, 1), 0.0),
+            )
+        return jnp.concatenate([left, right], 1).reshape(planes, rows, lanes)
+
+    def fine_left(x, which):
+        half = 6
+        blocks = cut_rows(x, 8, 16)
+        table = left_f[which]
+        return paste_rows(wide_left(table, blocks[:half]) + wide_left(table, blocks[half:]), 8)
+
+    def fine_pass(x, which, factor, result):
+        z = fine_left(fine_right(x, 2 * which, False), 2 * which)
+        z = z * factor[...]
+        result[...] = fine_left(fine_right(z, 2 * which + 1, True), 2 * which + 1)
 
     basis, basis_t = tables_of(bf_ref)
-    put_right(right_f, 0, right_table(basis, 8, 8))
-    put_left(left_f, 0, left_table(basis_t, 8, 8, 4))
-    put_right(right_f, 1, right_table(basis_t, 8, 8, joined=True, weighted=True))
-    put_left(left_f, 1, left_table(basis, 8, 8, 4, joined=True, weighted=True))
+
+    def put_fine(at, table, turned, weighted):
+        value = right_table(table, 8, 8, 16)
+        put_right(right_f, 4 * at, value)
+        put_right(right_f, 4 * at + 1, value)
+        put_left(left_f, 2 * at, left_table(turned, 8, 8, 2))
+        for end in range(2):
+            value = right_table(
+                turned, 8, 8, 16, joined=True, weighted=weighted, first=end == 0, last=end == 1
+            )
+            put_right(right_f, 4 * at + 2 + end, value)
+        put_left(left_f, 2 * at + 1, left_table(table, 8, 8, 2, joined=True, weighted=weighted))
+
+    put_fine(0, basis, basis_t, True)
     put_scales(scale_ref, ef_ref, 8, scale_f, inv_f)
 
     load_res.wait()
-    fine_pass(lambda a, g: cut(res, a, g)[...], 0, inv_f, first)
-    pl.semaphore_wait(barrier, devices - 1)
-    made = send_faces(0, 0, 8, first, 32, True)
+    fine_pass(res[...], 0, inv_f, first)
+    pl.semaphore_wait(barrier, greeted)
+    made = send_faces(0, 0, 8, first, 16, True)
 
     oper, oper_t = tables_of(qf_ref)
-    put_right(right_f, 2, right_table(oper, 8, 8))
-    put_left(left_f, 2, left_table(oper_t, 8, 8, 4))
-    put_right(right_f, 3, right_table(oper_t, 8, 8, joined=True))
-    put_left(left_f, 3, left_table(oper, 8, 8, 4, joined=True))
+    put_fine(1, oper, oper_t, False)
 
     join_faces(made, 0, 8, first, True)
-    fine_pass(lambda a, g: cut(first, a, g)[...], 1, scale_f, work)
-    made = send_faces(1, 1, 8, work, 32, False)
+    fine_pass(first[...], 1, scale_f, work)
+    made = send_faces(1, 1, 8, work, 16, False)
 
     put_scales(scale_ref, em_ref, 4, scale_m, inv_m)
-    pm, pm_t = tables_of(pm_ref)
-    put_right(right_rf, 0, right_table(pm, 4, 8, joined=True, weigh_input=True))
-    put_left(left_rf, 0, left_table(pm_t, 4, 8, 4, joined=True, weigh_input=True))
+    pm, pm_t = tables_of(pm_ref, True)
+    value = right_table(pm, 4, 8, joined=True, weigh_input=True)
+    put_right(right_rf, 0, value[:128])
+    put_right(right_rf, 1, value[128:])
+    put_left(left_rf, 0, left_table(pm_t, 4, 8, 2, joined=True, weigh_input=True))
+
+    def put_mid(at, table, turned, weighted):
+        put_right(right_m, 2 * at, right_table(table, 4, 4))
+        put_left_twice(left_m, 2 * at, left_table(turned, 4, 4, 4, copies=2))
+        put_right(right_m, 2 * at + 1, right_table(turned, 4, 4, joined=True, weighted=weighted))
+        value = left_table(table, 4, 4, 4, joined=True, weighted=weighted, copies=2)
+        put_left_twice(left_m, 2 * at + 1, value)
+
     basis, basis_t = tables_of(bm_ref)
-    put_pair(right_m, 0, right_table(basis, 4, 4))
-    put_pair(left_m, 0, left_table(basis_t, 4, 4, EZ))
-    put_pair(right_m, 1, right_table(basis_t, 4, 4, joined=True, weighted=True))
-    put_pair(left_m, 1, left_table(basis, 4, 4, EZ, joined=True, weighted=True))
+    put_mid(0, basis, basis_t, True)
 
     join_faces(made, 1, 8, work, False)
-    fine_pass(lambda a, g: cut(res, a, g)[...] - cut(work, a, g)[...], 0, inv_f, out_ref)
-    made = send_faces(2, 2, 8, out_ref, 32, True)
+    fine_pass(res[...] - work[...], 0, inv_f, second)
+    made = send_faces(2, 2, 8, second, 16, True)
 
     oper, oper_t = tables_of(qm_ref)
-    put_pair(right_m, 2, right_table(oper, 4, 4))
-    put_pair(left_m, 2, left_table(oper_t, 4, 4, EZ))
-    put_pair(right_m, 3, right_table(oper_t, 4, 4, joined=True))
-    put_pair(left_m, 3, left_table(oper, 4, 4, EZ, joined=True))
+    put_mid(1, oper, oper_t, False)
     put_scales(scale_ref, el_ref, 2, None, inv_l)
 
-    join_faces(made, 2, 8, out_ref, True)
-
-    def add_up(a, g):
-        total = cut(first, a, g)[...] + cut(out_ref, a, g)[...]
-        cut(first, a, g)[...] = total
-        return total
-
-    fine_pass(add_up, 1, scale_f, work)
-    made = send_faces(3, 3, 8, work, 32, False)
-
-    plow, plow_t = tables_of(plow_ref)
-    put_pair(right_rm, 0, right_table(plow, 2, 4, joined=True, weigh_input=True))
-    put_pair(left_rm, 0, left_table(plow_t, 2, 4, EZ, joined=True, weigh_input=True))
+    join_faces(made, 2, 8, second, True)
+    first[...] = first[...] + second[...]
+    fine_pass(first[...], 1, scale_f, work)
+    made = send_faces(3, 3, 8, work, 16, False)
+
+    plow, plow_t = tables_of(plow_ref, True)
+    value = right_table(plow, 2, 4, joined=True, weigh_input=True, copies=2)
+    high, low = split(value)
+    value = jnp.where(iota(value.shape, 1) < 64, high.astype(F32), low.astype(F32)).astype(BF)
+    right_rm[0, 0:128] = value
+    right_rm[0, 128:256] = value
+    value = left_table(plow_t, 2, 4, 4, joined=True, weigh_input=True, copies=2)
+    put_left_twice(left_rm, 0, value)
     basis, basis_t = tables_of(bl_ref)
     put_pair(right_l, 0, right_table(basis, 2, 2))
     put_pair(left_l, 0, left_table(basis_t, 2, 2, EZ))
@@ -411,17 +486,22 @@
 
     join_faces(made, 3, 8, work, False)
 
-    def restrict(a, g):
-        x = cut(res, a, g)[...] - cut(work, a, g)[...]
-        low = jnp.where(a == 0, weight_low_end, 0.5)
-        high = jnp.where(a == 0, 0.5, weight_high_end)
-        x = jnp.concatenate([x[0:1] * low, x[1:7], x[7:8] * high], 0)
-        y = stacked_right(x.reshape(256, 256), right_rf[0])
-        z = stacked_left(left_rf[0], y)
-        cut(rhs_m, a, g, 4, 16)[...] = z.reshape(4, 16, 128)
-
-    fine_loop(restrict)
-    made = send_faces(4, 0, 4, rhs_m, 16, False)
+    def ends_weighed(x, n):
+        planes = x.shape[0]
+        return jnp.concatenate(
+            [
+                x[0:1] * weight_low_end, x[1 : n - 1], x[n - 1 : n + 1] * 0.5,
+                x[n + 1 : planes - 1], x[planes - 1 :] * weight_high_end,
+            ],
+            0,
+        )
+
+    blocks = cut_rows(ends_weighed(res[...] - work[...], 8), 8, 16)
+    x = paste_rows(wide_left(left_rf[0], blocks[:6]) + wide_left(left_rf[0], blocks[6:]), 4)
+    x = x.reshape(384, 256)
+    x = wide_right(x[:, :128], right_rf[0]) + wide_right(x[:, 128:], right_rf[1])
+    rhs_m[...] = x.reshape(8, 48, 128)
+    made = send_faces(4, 0, 4, rhs_m, 8, False)
 
     route = route_ref[...]
     hot = picked(iota((64, 768), 0) == route)
@@ -430,48 +510,42 @@
     rank = jnp.sum(mm(target_hot[...], earlier) * hot, axis=0, keepdims=True)
     slot_hot[...] = picked(iota((128, 768), 0).astype(F32) == rank)
     half = jnp.where(rank >= HALF_CAP, 1.0, 0.0)
-    owner = 2.0 * route.astype(F32) + half
-    row_hot[...] = picked(iota((128, 768), 0).astype(F32) == owner).astype(BF)
+    owner = 2 * route + jnp.where(rank >= HALF_CAP, 1, 0)
+    owner = lax.rem(owner, n_azim) * n_axial + owner // n_azim
+    row_hot[...] = picked(iota((128, 768), 0) == owner).astype(BF)
     place_hot[...] = picked(iota((16, 768), 0).astype(F32) == rank - HALF_CAP * half)
 
     join_faces(made, 0, 4, rhs_m, False)
 
-    def small_pass(x, n, right, left, which, factor):
-        planes, rows, lanes = x.shape
-        for side in range(2):
-            y = mm_right(x.reshape(planes * rows, lanes), right.at[2 * which + side])
-            y = y.reshape(2, n * rows, lanes)
-            z = [mm_left(left.at[2 * which + side], y[a]) for a in range(2)]
-            x = jnp.concatenate([v.reshape(n, rows, lanes) for v in z], 0)
-            if side == 0:
+    def mid_pass(x, which, factor):
+        for at in (2 * which, 2 * which + 1):
+            x = wide_right(x.reshape(384, 128), right_m[at]).reshape(8, 48, 128)
+            x = paste_rows(wide_left(left_m[at], cut_rows(x, 4, 16)), 4)
+            if at == 2 * which:
                 x = x * factor[...]
         return x
 
-    smooth_m[...] = small_pass(rhs_m[...], 4, right_m, left_m, 0, inv_m)
-    made = send_faces(5, 1, 4, smooth_m, None, True)
+    smooth_m[...] = mid_pass(rhs_m[...], 0, inv_m)
+    made = send_faces(5, 1, 4, smooth_m, 16, True)
     put_right(right_pf, 0, right_table(pm_t, 8, 4))
-    put_pair(left_pf, 0, left_table(pm, 8, 4, 4))
+    put_left_thrice(left_pf, 0, left_table(pm, 8, 4, 4, copies=3))
     join_faces(made, 1, 4, smooth_m, True)
 
-    work_m[...] = small_pass(smooth_m[...], 4, right_m, left_m, 1, scale_m)
-    made = send_faces(6, 2, 4, work_m, None, False)
+    work_m[...] = mid_pass(smooth_m[...], 1, scale_m)
+    made = send_faces(6, 2, 4, work_m, 16, False)
     both = jnp.zeros((8, 128), F32)
     both_t = jnp.zeros((8, 128), F32)
     for k in range(4):
         both = both + pm[:, k : k + 1] * plow[k : k + 1, :]
         both_t = both_t + plow_t[:, k : k + 1] * pm_t[k : k + 1, :]
     put_pair(right_pp, 0, right_table(both_t, 8, 2))
-    put_pair(left_pp, 0, left_table(both, 8, 2, 4))
+    put_left_thrice(left_pp, 0, left_table(both, 8, 2, 4, copies=3))
     join_faces(made, 2, 4, work_m, False)
 
-    x = rhs_m[...] - work_m[...]
-    x = jnp.concatenate(
-        [x[0:1] * weight_low_end, x[1:3], x[3:5] * 0.5, x[5:7], x[7:8] * weight_high_end], 0
-    )
-    y = mm_right(x.reshape(384, 128), right_rm.at[0]).reshape(2, 192, 64)
-    for a in range(2):
-        rhs_l[2 * a : 2 * a + 2] = mm_left(left_rm.at[0], y[a]).reshape(2, 24, 64)
-    made = send_faces(7, 0, 2, rhs_l, None, False)
+    blocks = cut_rows(ends_weighed(rhs_m[...] - work_m[...], 4), 4, 16)
+    x = paste_rows(wide_left(left_rm[0], blocks), 2).reshape(96, 128)
+    rhs_l[...] = wide_right(x, right_rm[0]).reshape(4, 24, 64)
+    made = send_faces(7, 0, 2, rhs_l, 8, False)
 
     slot = iota((128, 3072), 0)
     lane = iota((1, 3072), 1)
@@ -496,42 +570,60 @@
         target_hot[...], high, nt, preferred_element_type=F32
     ) + lax.dot_general(target_hot[...], low, nt, preferred_element_type=F32)
     for t in range(64):
-        send_a[t] = flat_a[t : t + 1]
-
-    def spread_out(source_of, target, sem, row_of):
+        send_a[t % 2, t // 2] = flat_a[t : t + 1]
+
+    def across(count, copy_to, sem):
         def start(j, carry):
-            other = lax.rem(me + j, devices)
+            source, target, device = copy_to(j)
             pltpu.make_async_remote_copy(
-                src_ref=source_of.at[row_of(other)], dst_ref=target.at[me],
+                src_ref=source, dst_ref=target,
                 send_sem=all_sem.at[sem], recv_sem=all_sem.at[sem + 1],
-                device_id=device_of(other), device_id_type=MESH,
+                device_id=device, device_id_type=MESH,
             ).start()
             return carry
 
-        lax.fori_loop(1, devices, start, 0)
-        target[me] = source_of[row_of(me)]
-
-    def wait_all(target, sem):
-        some = target.at[pl.ds(0, devices - 1)]
+        lax.fori_loop(1, count, start, 0)
+
+    def wait_all(target, count, sem):
+        some = target.at[pl.ds(0, count - 1)]
         pltpu.make_async_copy(some, some, all_sem.at[sem]).wait()
 
-    spread_out(send_a, recv_a, 0, lambda other: other // 2)
-
-    smooth_l[...] = small_pass(rhs_l[...], 2, right_l, left_l, 0, inv_l)
+    def first_out(j):
+        other = lax.rem(me_z + j, n_azim)
+        return send_a.at[other // 2], stage_a.at[me_z], (me_a, other)
+
+    across(n_azim, first_out, 0)
+    stage_a[me_z] = send_a[me_z // 2]
+
+    def low_pass(x, factor):
+        for side in range(2):
+            y = mm_right(x.reshape(96, 64), right_l.at[side]).reshape(2, 48, 64)
+            x = jnp.concatenate(
+                [mm_left(left_l.at[side], y[a]).reshape(2, 24, 64) for a in range(2)], 0
+            )
+            if side == 0:
+                x = x * factor[...]
+        return x
+
+    smooth_l[...] = low_pass(rhs_l[...], inv_l)
     made = send_faces(8, 1, 2, smooth_l, None, True)
-
-    def prolong(a, g):
-        x = cut(smooth_m, a, g, 4, 16)[...].reshape(64, 128)
-        y = stacked_right(x, right_pf[0])
-        z = mm_left(left_pf.at[0], y)
-        cut(out_ref, a, g)[...] = cut(first, a, g)[...] + z.reshape(8, 32, 256)
-
-    fine_loop(prolong)
+    wait_all(stage_a, n_azim, 1)
+
+    def second_out(j):
+        other = lax.rem(me_a + j, n_axial)
+        return stage_a.at[:, other], recv_a.at[me_a], (other, me_z)
+
+    across(n_axial, second_out, 2)
+    recv_a[me_a] = stage_a[:, me_a]
+
+    x = wide_right(smooth_m[...].reshape(384, 128), right_pf[0]).reshape(8, 48, 256)
+    x = paste_rows(thrice_left(left_pf[0], cut_rows(x, 4, 16)), 8)
+    out_ref[...] = first[...] + x
     join_faces(made, 1, 2, smooth_l, True)
 
-    wait_all(recv_a, 1)
+    wait_all(recv_a, n_axial, 3)
     for d in range(devices):
-        flat_b[d : d + 1] = recv_a[d]
+        flat_b[d : d + 1] = recv_a[d // n_azim, d % n_azim]
     high, low = split(flat_b[...])
     wide = mm(high, sel_hot[...]) + mm(low, sel_hot[...])
     wide = jnp.where(iota((128, 3072), 0) == source, wide, 0.0)
@@ -563,11 +655,25 @@
     gather = picked(iota((128, 1536), 0) == group).astype(BF)
     flat_b[...] = mm(gather, high) + mm(gather, low)
     for d in range(devices):
-        send_b[d] = flat_b[d : d + 1]
-    spread_out(send_b, recv_b, 2, lambda other: other)
-    wait_all(recv_b, 3)
+        send_b[d // n_azim, d % n_azim] = flat_b[d : d + 1]
+
+    def first_back(j):
+        other = lax.rem(me_a + j, n_axial)
+        return send_b.at[other], stage_b.at[me_a], (other, me_z)
+
+    across(n_axial, first_back, 4)
+    stage_b[me_a] = send_b[me_a]
+    wait_all(stage_b, n_axial, 5)
+
+    def second_back(j):
+        other = lax.rem(me_z + j, n_azim)
+        return stage_b.at[:, other], recv_b.at[me_z], (me_a, other)
+
+    across(n_azim, second_back, 6)
+    recv_b[me_z] = stage_b[:, me_z]
+    wait_all(recv_b, n_azim, 7)
     for d in range(devices):
-        flat_b[d : d + 1] = recv_b[d]
+        flat_b[d : d + 1] = recv_b[d // n_axial, d % n_axial]
 
     turned = jnp.transpose(flat_b[...])[0:16]
     high, low = split(turned)
@@ -611,24 +717,20 @@
     total_l[3] = smooth_l[3] + beyond
 
     wide = mm_right(total_l[...].reshape(96, 64), right_pp.at[0]).reshape(4, 24, 256)
-    for a in range(2):
-        for g in range(3):
-            x = wide[2 * a : 2 * a + 2, 8 * g : 8 * g + 8].reshape(16, 256)
-            z = mm_left(left_pp.at[0], x).reshape(8, 32, 256)
-            out_ref[8 * a : 8 * a + 8, 32 * g : 32 * g + 32] += z
+    out_ref[...] += paste_rows(thrice_left(left_pp[0], cut_rows(wide, 2, 8)), 8)
 
     for copy in pending:
         copy.wait_send()
-    wait_all(recv_a, 0)
-    wait_all(recv_b, 2)
+    wait_all(stage_a, n_azim, 0)
+    wait_all(recv_a, n_axial, 2)
+    wait_all(stage_b, n_axial, 4)
+    wait_all(recv_b, n_azim, 6)
 
 
 def on_device(
     residual, element_scale, basis_fine, eigen_fine, operator_fine, basis_mid, eigen_mid,
     operator_mid, basis_low, eigen_low, prolong_mid, prolong_low, vertex_route, coarse_inverse,
 ):
-    devices = lax.axis_size("axial") * lax.axis_size("azim")
-
     def vm(*shape, dtype=F32):
         return pltpu.VMEM(shape, dtype)
 
@@ -641,24 +743,24 @@
 
     fine, mid, low = (16, 96, 256), (8, 48, 128), (4, 24, 64)
     scratch = [
-        vm(*fine), vm(*fine), vm(*fine), vm(*fine), vm(*fine),
+        vm(*fine), vm(*fine), vm(*fine), vm(*fine), vm(*fine), vm(*fine),
         vm(*mid), vm(*mid), vm(*mid), vm(*mid), vm(*mid),
         vm(*low), vm(*low), vm(*low), vm(*low),
-        vm(4, 768, 256, dtype=BF), vm(4, 256, 768, dtype=BF),
-        vm(1, 768, 128, dtype=BF), vm(1, 64, 768, dtype=BF),
-        vm(1, 384, 256, dtype=BF), vm(1, 2, 256, 64, dtype=BF),
-        vm(4, 2, 128, 128, dtype=BF), vm(4, 2, 192, 192, dtype=BF),
-        vm(1, 2, 128, 64, dtype=BF), vm(1, 2, 48, 192, dtype=BF),
+        vm(8, 256, 256, dtype=BF), vm(4, 256, 256, dtype=BF),
+        vm(2, 256, 256, dtype=BF), vm(1, 64, 256, dtype=BF),
+        vm(1, 256, 512, dtype=BF), vm(1, 256, 192, dtype=BF),
+        vm(4, 256, 256, dtype=BF), vm(4, 128, 128, dtype=BF),
+        vm(1, 256, 128, dtype=BF), vm(1, 32, 128, dtype=BF),
         vm(2, 2, 64, 64, dtype=BF), vm(2, 2, 48, 48, dtype=BF),
-        vm(1, 2, 64, 256, dtype=BF), vm(1, 2, 256, 16, dtype=BF),
+        vm(1, 2, 64, 256, dtype=BF), vm(1, 256, 48, dtype=BF),
         vm(1536, 3072), vm(64, 768, dtype=BF), vm(128, 768), vm(128, 768, dtype=BF),
         vm(16, 768), vm(128, 3072, dtype=BF), vm(8, 3072), vm(1536, 128),
-        vm(64, 128), vm(64, 1, 128), vm(devices, 1, 128),
-        vm(devices, 128), vm(devices, 1, 128), vm(devices, 1, 128),
+        vm(64, 128), vm(2, 32, 1, 128), vm(4, 32, 1, 128), vm(32, 4, 1, 128),
+        vm(128, 128), vm(32, 4, 1, 128), vm(32, 4, 1, 128), vm(4, 32, 1, 128),
         vm(24, 64), vm(2, 1, 64), vm(24, 64), vm(3, 1, 64),
         *face_buffers(4, *fine), *face_buffers(3, *mid), *face_buffers(2, *low),
         pltpu.SemaphoreType.DMA((10, 8)), pltpu.SemaphoreType.DMA((10, 8)),
-        pltpu.SemaphoreType.DMA((2,)), pltpu.SemaphoreType.DMA((4,)),
+        pltpu.SemaphoreType.DMA((2,)), pltpu.SemaphoreType.DMA((8,)),
     ]
     in_vmem = pl.BlockSpec(memory_space=pltpu.VMEM)
     in_smem = pl.BlockSpec(memory_space=pltpu.SMEM)
@@ -679,9 +781,9 @@
         ),
     )
     return call(
-        residual, element_scale, vertex_route.reshape(1, -1), coarse_inverse,
+        residual, jnp.transpose(element_scale, (0, 2, 1, 3)), vertex_route.reshape(1, -1), coarse_inverse,
         basis_fine, eigen_fine, operator_fine, basis_mid, eigen_mid, operator_mid,
-        basis_low, eigen_low, prolong_mid, prolong_low,
+        basis_low, eigen_low, prolong_mid.T, prolong_low.T,
     )
 
 

time: 118 us -> 89.7 us (0.76)
  Pallas kernels: 111 us -> 86.8 us
  local copies, waits for them, and re-layouts: 6.76 us -> 2.69 us
    pallas_call x1, Pallas kernels: 111 us -> 86.8 us  [on_device(): call(residual, jnp.transpose(element_scale, (0, 2, 1, 3)), vertex_route.r...]
    unnamed x4 -> x1, local copies, waits for them, and re-layouts: 6.76 us -> 2.69 us
where the time goes in v1:
time: 89.7 us; the launch traced here: 89.5 us
  Pallas kernels  86.8 us (97%)
  local copies, waits for them, and re-layouts  2.69 us (3%)
    pallas_call x1, Pallas kernels, on_device(): call(residual, jnp.transpose(element_scale, (0, 2, 1, 3)), vertex_route.r...  86.8 us
    unnamed x1, local copies, waits for them, and re-layouts  2.69 us

profile of v1, /device:TPU:1, one launch (start us, length us, event | category | flops | bytes accessed | tf_op | source)
XLA Modules:
  0.0 89.5 jit_solution(5555426866724741327)
XLA Ops:
  0.0 86.8 %shard_map.136 = f32[16,96,256]{2,1,0:T(8,128)} custom-call(f32[16,96,256]{2,1,0:T(8,128)} %res_hbm.1, f32[3,12,2,32]{3,2,1,0:T(2,128)} %bitcast.4, s32[1,768]{1,0:T(1,128)} %bitcast.5, f32[1,1,1536,3072]{3,2,1,0:T(8,128)} %inverse_hbm.1, f32[8,8]{1,0:T(8,128)} %bf_ref.1, f32[8]{0:T(128)} %ef_ref.1, f32[8,8]{1,0:T(8,128)} %qf_ref.1, f32[4,4]{1,0:T(4,128)} %bm_ref.1, ...), custom_call_target="tpu_custom_call" | custom-call | flops 12000000000 | bytes 24000000 | tf_op jit(solution)/shard_map/pallas_call | solution.py:783
  86.8 2.7 %copy.16 = f32[16,96,256]{2,1,0:T(8,128)} copy(f32[16,96,256]{2,1,0:T(8,128)} %shard_map.136) | data formatting | bytes 3145728

commit v2 on v1

--- a/solution.py
+++ b/solution.py
@@ -269,15 +269,17 @@
     right_f, left_f, right_rf, left_rf, right_pf, left_pf,
     right_m, left_m, right_rm, left_rm, right_l, left_l, right_pp, left_pp,
     dense, target_hot, slot_hot, row_hot, place_hot, sel_hot, vector, partial,
-    flat_a, send_a, stage_a, recv_a, flat_b, send_b, stage_b, recv_b, cs_plane, cs_row, cr_plane, cr_row,
+    flat_a, send_a, recv_a, flat_b, send_b, recv_b, cs_plane, cs_row, cr_plane, cr_row,
+    hold_f, hold_m, hold_l,
     fs_ax, fr_ax, fs_az, fr_az, fs_dg, fr_dg,
     ms_ax, mr_ax, ms_az, mr_az, ms_dg, mr_dg,
     ls_ax, lr_ax, ls_az, lr_az, ls_dg, lr_dg,
-    send_sem, recv_sem, load_sem, all_sem,
+    send_sem, recv_sem, load_sem, all_sem, word_sem,
     *, n_axial, n_azim,
 ):
     devices = n_axial * n_azim
     me_a, me_z = lax.axis_index("axial"), lax.axis_index("azim")
+    me = me_a * n_azim + me_z
 
     def neighbour(da, dz):
         return (lax.rem(me_a + n_axial + da, n_axial), lax.rem(me_z + n_azim + dz, n_azim))
@@ -289,25 +291,20 @@
 
     barrier = pltpu.get_barrier_semaphore()
 
-    def greet(device):
-        pl.semaphore_signal(barrier, inc=1, device_id=device, device_id_type=MESH)
-
-    def along(j):
-        return (lax.rem(me_a + j, n_axial), me_z)
-
-    def around(j):
-        return (me_a, lax.rem(me_z + j, n_azim))
-
-    def greet_along(j, carry):
-        greet(along(j))
-        return carry
-
+    for j in range(1, n_axial):
+        other = (lax.rem(me_a + j, n_axial), me_z)
+        pl.semaphore_signal(barrier, inc=1, device_id=other, device_id_type=MESH)
+    for j in range(1, n_azim):
+        other = (me_a, lax.rem(me_z + j, n_azim))
+        pl.semaphore_signal(barrier, inc=1, device_id=other, device_id_type=MESH)
     for da, dz in DIRS[4:]:
-        greet(neighbour(da, dz))
-    for j in range(1, n_azim):
-        greet(around(j))
-    lax.fori_loop(1, n_axial, greet_along, 0)
-    greeted = 4 + n_azim - 1 + n_axial - 1
+        pl.semaphore_signal(barrier, inc=1, device_id=neighbour(da, dz), device_id_type=MESH)
+
+    def spread_word():
+        pl.semaphore_wait(barrier, n_axial - 1 + n_azim - 1 + 4)
+        for j in range(1, n_azim):
+            other = (me_a, lax.rem(me_z + j, n_azim))
+            pl.semaphore_signal(word_sem, inc=1, device_id=other, device_id_type=MESH)
 
     first_device, last_device = me_a == 0, me_a == n_axial - 1
     weight_low_end = jnp.where(first_device, 1.0, 0.5).astype(F32)
@@ -362,15 +359,15 @@
             s_az[slot, 0, i : i + 1] = buf[i, rows - 1 : rows]
             s_az[slot, 1, i : i + 1] = buf[i, 0:1]
         made = copies_of(e, slot, n)
-        for copy in made:
+        for copy in made[4:] + made[:4]:
             copy.start()
         pending.extend(made)
         return made
 
     def join_faces(made, slot, n, buf, weighted):
         planes, rows, _ = buf.shape
-        _, r_ax, _, r_az, _, r_dg = faces[n]
-        for copy in made:
+        _, r_ax, _, r_az, _, _ = faces[n]
+        for copy in made[:4]:
             copy.wait_recv()
         for i in range(planes):
             buf[i, 0:1] = buf[i, 0:1] + r_az[slot, 0, i : i + 1]
@@ -379,13 +376,37 @@
             (0, 0, first_device, weight_low_end),
             (1, planes - 1, last_device, weight_high_end),
         ):
-            buf[plane] = buf[plane] + jnp.where(device, 0.0, r_ax[slot, end])
-            buf[plane, 0:1] = buf[plane, 0:1] + jnp.where(device, 0.0, r_dg[slot, 2 * end])
-            buf[plane, rows - 1 : rows] = buf[plane, rows - 1 : rows] + jnp.where(
-                device, 0.0, r_dg[slot, 2 * end + 1]
-            )
+            total = buf[plane] + jnp.where(device, 0.0, r_ax[slot, end])
+            buf[plane] = total * weight if weighted else total
+
+    def join_corners(made, slot, n, buf, weighted):
+        r_dg, hold = faces[n][5], holds[n]
+        for copy in made[4:]:
+            copy.wait_recv()
+        for k in range(4):
+            end = k // 2
+            line = jnp.where((first_device, last_device)[end], 0.0, r_dg[slot, k])
             if weighted:
-                buf[plane] = buf[plane] * weight
+                line = line * (weight_low_end, weight_high_end)[end]
+            hold[k : k + 1] = line
+            if buf is not None:
+                plane, row = (0, buf.shape[0] - 1)[end], (0, buf.shape[1] - 1)[k % 2]
+                buf[plane, row : row + 1] = buf[plane, row : row + 1] + line
+        return hold[...]
+
+    def add_corners(blocks, table, columns, lines):
+        half, count = table.shape[0] // 2, len(blocks) // 2
+        table = table[:, :128].astype(F32)
+        for k, column in enumerate(columns):
+            at = (0, count - 1, count, 2 * count - 1)[k]
+            factor = table[:half, column : column + 1] + table[half:, column : column + 1]
+            blocks[at] = blocks[at] + factor * lines[k : k + 1]
+        return blocks
+
+    FINE_CORNERS, MID_CORNERS = (0, 15, 112, 127), (0, 15, 48, 63)
+    holds = {8: hold_f, 4: hold_m, 2: hold_l}
+    for hold in holds.values():
+        hold[...] = jnp.zeros(hold.shape, F32)
 
     def fine_right(x, which, joined):
         planes, rows, lanes = x.shape
@@ -404,12 +425,16 @@
         half = 6
         blocks = cut_rows(x, 8, 16)
         table = left_f[which]
-        return paste_rows(wide_left(table, blocks[:half]) + wide_left(table, blocks[half:]), 8)
-
-    def fine_pass(x, which, factor, result):
+        return wide_left(table, blocks[:half]) + wide_left(table, blocks[half:])
+
+    def fine_pass(x, which, factor, result, corners=None):
         z = fine_left(fine_right(x, 2 * which, False), 2 * which)
-        z = z * factor[...]
-        result[...] = fine_left(fine_right(z, 2 * which + 1, True), 2 * which + 1)
+        if corners is not None:
+            lines = fine_right(corners().reshape(1, 16, 256), 2 * which, False).reshape(16, 256)
+            z = add_corners(z, left_f[2 * which], FINE_CORNERS, lines)
+        z = paste_rows(z, 8) * factor[...]
+        z = fine_right(z, 2 * which + 1, True)
+        result[...] = paste_rows(fine_left(z, 2 * which + 1), 8)
 
     basis, basis_t = tables_of(bf_ref)
 
@@ -430,14 +455,16 @@
 
     load_res.wait()
     fine_pass(res[...], 0, inv_f, first)
-    pl.semaphore_wait(barrier, greeted)
+    spread_word()
     made = send_faces(0, 0, 8, first, 16, True)
 
     oper, oper_t = tables_of(qf_ref)
     put_fine(1, oper, oper_t, False)
 
     join_faces(made, 0, 8, first, True)
-    fine_pass(first[...], 1, scale_f, work)
+    fine_pass(
+        first[...], 1, scale_f, work, lambda: join_corners(made, 0, 8, first, True)
+    )
     made = send_faces(1, 1, 8, work, 16, False)
 
     put_scales(scale_ref, em_ref, 4, scale_m, inv_m)
@@ -458,7 +485,9 @@
     put_mid(0, basis, basis_t, True)
 
     join_faces(made, 1, 8, work, False)
-    fine_pass(res[...] - work[...], 0, inv_f, second)
+    fine_pass(
+        res[...] - work[...], 0, inv_f, second, lambda: -join_corners(made, 1, 8, work, False)
+    )
     made = send_faces(2, 2, 8, second, 16, True)
 
     oper, oper_t = tables_of(qm_ref)
@@ -467,7 +496,9 @@
 
     join_faces(made, 2, 8, second, True)
     first[...] = first[...] + second[...]
-    fine_pass(first[...], 1, scale_f, work)
+    fine_pass(
+        first[...], 1, scale_f, work, lambda: join_corners(made, 2, 8, first, True)
+    )
     made = send_faces(3, 3, 8, work, 16, False)
 
     plow, plow_t = tables_of(plow_ref, True)
@@ -497,7 +528,9 @@
         )
 
     blocks = cut_rows(ends_weighed(res[...] - work[...], 8), 8, 16)
-    x = paste_rows(wide_left(left_rf[0], blocks[:6]) + wide_left(left_rf[0], blocks[6:]), 4)
+    blocks = wide_left(left_rf[0], blocks[:6]) + wide_left(left_rf[0], blocks[6:])
+    lines = -join_corners(made, 3, 8, None, True)
+    x = paste_rows(add_corners(blocks, left_rf[0], FINE_CORNERS, lines), 4)
     x = x.reshape(384, 256)
     x = wide_right(x[:, :128], right_rf[0]) + wide_right(x[:, 128:], right_rf[1])
     rhs_m[...] = x.reshape(8, 48, 128)
@@ -511,27 +544,34 @@
     slot_hot[...] = picked(iota((128, 768), 0).astype(F32) == rank)
     half = jnp.where(rank >= HALF_CAP, 1.0, 0.0)
     owner = 2 * route + jnp.where(rank >= HALF_CAP, 1, 0)
-    owner = lax.rem(owner, n_azim) * n_axial + owner // n_azim
     row_hot[...] = picked(iota((128, 768), 0) == owner).astype(BF)
     place_hot[...] = picked(iota((16, 768), 0).astype(F32) == rank - HALF_CAP * half)
 
     join_faces(made, 0, 4, rhs_m, False)
 
-    def mid_pass(x, which, factor):
-        for at in (2 * which, 2 * which + 1):
-            x = wide_right(x.reshape(384, 128), right_m[at]).reshape(8, 48, 128)
-            x = paste_rows(wide_left(left_m[at], cut_rows(x, 4, 16)), 4)
-            if at == 2 * which:
-                x = x * factor[...]
-        return x
-
-    smooth_m[...] = mid_pass(rhs_m[...], 0, inv_m)
+    def mid_right(x, at):
+        planes, rows, lanes = x.shape
+        return wide_right(x.reshape(planes * rows, lanes), right_m[at]).reshape(x.shape)
+
+    def mid_pass(x, which, factor, corners):
+        at = 2 * which
+        blocks = wide_left(left_m[at], cut_rows(mid_right(x, at), 4, 16))
+        lines = mid_right(corners().reshape(1, 16, 128), at).reshape(16, 128)
+        x = paste_rows(add_corners(blocks, left_m[at], MID_CORNERS, lines), 4) * factor[...]
+        x = mid_right(x, at + 1)
+        return paste_rows(wide_left(left_m[at + 1], cut_rows(x, 4, 16)), 4)
+
+    smooth_m[...] = mid_pass(
+        rhs_m[...], 0, inv_m, lambda: join_corners(made, 0, 4, rhs_m, False)
+    )
     made = send_faces(5, 1, 4, smooth_m, 16, True)
     put_right(right_pf, 0, right_table(pm_t, 8, 4))
     put_left_thrice(left_pf, 0, left_table(pm, 8, 4, 4, copies=3))
     join_faces(made, 1, 4, smooth_m, True)
 
-    work_m[...] = mid_pass(smooth_m[...], 1, scale_m)
+    work_m[...] = mid_pass(
+        smooth_m[...], 1, scale_m, lambda: join_corners(made, 1, 4, smooth_m, True)
+    )
     made = send_faces(6, 2, 4, work_m, 16, False)
     both = jnp.zeros((8, 128), F32)
     both_t = jnp.zeros((8, 128), F32)
@@ -543,7 +583,9 @@
     join_faces(made, 2, 4, work_m, False)
 
     blocks = cut_rows(ends_weighed(rhs_m[...] - work_m[...], 4), 4, 16)
-    x = paste_rows(wide_left(left_rm[0], blocks), 2).reshape(96, 128)
+    blocks = wide_left(left_rm[0], blocks)
+    lines = -join_corners(made, 2, 4, None, True)
+    x = paste_rows(add_corners(blocks, left_rm[0], MID_CORNERS, lines), 2).reshape(96, 128)
     rhs_l[...] = wide_right(x, right_rm[0]).reshape(4, 24, 64)
     made = send_faces(7, 0, 2, rhs_l, 8, False)
 
@@ -555,6 +597,7 @@
     wanted = half_lane * HALF_CAP + rest - source * HALF_CAP
     sel_hot[...] = picked(slot == wanted).astype(BF)
     join_faces(made, 0, 2, rhs_l, False)
+    join_corners(made, 0, 2, rhs_l, False)
 
     values = []
     lane = iota((24, 384), 1)
@@ -570,30 +613,35 @@
         target_hot[...], high, nt, preferred_element_type=F32
     ) + lax.dot_general(target_hot[...], low, nt, preferred_element_type=F32)
     for t in range(64):
-        send_a[t % 2, t // 2] = flat_a[t : t + 1]
-
-    def across(count, copy_to, sem):
-        def start(j, carry):
-            source, target, device = copy_to(j)
+        send_a[t] = flat_a[t : t + 1]
+
+    def spread_out(source, row_of, target, sem):
+        def start(a, z):
             pltpu.make_async_remote_copy(
-                src_ref=source, dst_ref=target,
+                src_ref=source.at[row_of(a, z)], dst_ref=target.at[me],
                 send_sem=all_sem.at[sem], recv_sem=all_sem.at[sem + 1],
-                device_id=device, device_id_type=MESH,
+                device_id=(a, z), device_id_type=MESH,
             ).start()
+
+        around = [lax.rem(me_z + j, n_azim) for j in range(n_azim)]
+
+        def start_line(j, carry):
+            a = lax.rem(me_a + j, n_axial)
+            for z in around:
+                start(a, z)
             return carry
 
-        lax.fori_loop(1, count, start, 0)
-
-    def wait_all(target, count, sem):
-        some = target.at[pl.ds(0, count - 1)]
+        lax.fori_loop(1, n_axial, start_line, 0)
+        for z in around[1:]:
+            start(me_a, z)
+        target[me] = source[row_of(me_a, me_z)]
+
+    def wait_all(target, sem):
+        some = target.at[pl.ds(0, devices - 1)]
         pltpu.make_async_copy(some, some, all_sem.at[sem]).wait()
 
-    def first_out(j):
-        other = lax.rem(me_z + j, n_azim)
-        return send_a.at[other // 2], stage_a.at[me_z], (me_a, other)
-
-    across(n_azim, first_out, 0)
-    stage_a[me_z] = send_a[me_z // 2]
+    pl.semaphore_wait(word_sem, n_azim - 1)
+    spread_out(send_a, lambda a, z: a * (n_azim // 2) + z // 2, recv_a, 0)
 
     def low_pass(x, factor):
         for side in range(2):
@@ -607,25 +655,11 @@
 
     smooth_l[...] = low_pass(rhs_l[...], inv_l)
     made = send_faces(8, 1, 2, smooth_l, None, True)
-    wait_all(stage_a, n_azim, 1)
-
-    def second_out(j):
-        other = lax.rem(me_a + j, n_axial)
-        return stage_a.at[:, other], recv_a.at[me_a], (other, me_z)
-
-    across(n_axial, second_out, 2)
-    recv_a[me_a] = stage_a[:, me_a]
-
-    x = wide_right(smooth_m[...].reshape(384, 128), right_pf[0]).reshape(8, 48, 256)
-    x = paste_rows(thrice_left(left_pf[0], cut_rows(x, 4, 16)), 8)
-    out_ref[...] = first[...] + x
-    join_faces(made, 1, 2, smooth_l, True)
-
-    wait_all(recv_a, n_axial, 3)
+    wait_all(recv_a, 1)
     for d in range(devices):
-        flat_b[d : d + 1] = recv_a[d // n_azim, d % n_azim]
-    high, low = split(flat_b[...])
-    wide = mm(high, sel_hot[...]) + mm(low, sel_hot[...])
+        flat_b[d : d + 1] = recv_a[d]
+    wide = mm(jnp.concatenate(split(flat_b[...]), 0), sel_hot[...])
+    wide = wide[:devices] + wide[devices:]
     wide = jnp.where(iota((128, 3072), 0) == source, wide, 0.0)
     vector[...] = jnp.broadcast_to(jnp.sum(wide, axis=0, keepdims=True), (8, 3072))
     load_dense.wait()
@@ -643,37 +677,28 @@
         return carry
 
     lax.fori_loop(0, 48, rows_of, 0)
-    high, low = split(partial[...])
-    ones = jnp.ones((128, 128), BF)
-    sums = mm(high, ones) + mm(low, ones)
+    sums = mm(jnp.concatenate(split(partial[...]), 1), jnp.ones((256, 128), BF))
     row = iota((1536, 128), 0)
     group = jnp.floor((row.astype(F32) + 0.5) * (1.0 / HALF_CAP)).astype(jnp.int32)
     sums = jnp.where(iota((1536, 128), 1) == row - group * HALF_CAP, sums, 0.0)
-    high, low = split(sums)
     lane = iota((1, 1536), 1)
     group = jnp.floor((lane.astype(F32) + 0.5) * (1.0 / HALF_CAP)).astype(jnp.int32)
     gather = picked(iota((128, 1536), 0) == group).astype(BF)
-    flat_b[...] = mm(gather, high) + mm(gather, low)
+    both = mm(gather, jnp.concatenate(split(sums), 1))
+    flat_b[...] = both[:, :128] + both[:, 128:]
     for d in range(devices):
-        send_b[d // n_azim, d % n_azim] = flat_b[d : d + 1]
-
-    def first_back(j):
-        other = lax.rem(me_a + j, n_axial)
-        return send_b.at[other], stage_b.at[me_a], (other, me_z)
-
-    across(n_axial, first_back, 4)
-    stage_b[me_a] = send_b[me_a]
-    wait_all(stage_b, n_axial, 5)
-
-    def second_back(j):
-        other = lax.rem(me_z + j, n_azim)
-        return stage_b.at[:, other], recv_b.at[me_z], (me_a, other)
-
-    across(n_azim, second_back, 6)
-    recv_b[me_z] = stage_b[:, me_z]
-    wait_all(recv_b, n_azim, 7)
+        send_b[d] = flat_b[d : d + 1]
+    spread_out(send_b, lambda a, z: a * n_azim + z, recv_b, 2)
+
+    x = wide_right(smooth_m[...].reshape(384, 128), right_pf[0]).reshape(8, 48, 256)
+    x = paste_rows(thrice_left(left_pf[0], cut_rows(x, 4, 16)), 8)
+    out_ref[...] = first[...] + x
+    join_faces(made, 1, 2, smooth_l, True)
+    join_corners(made, 1, 2, smooth_l, True)
+
+    wait_all(recv_b, 3)
     for d in range(devices):
-        flat_b[d : d + 1] = recv_b[d // n_axial, d % n_axial]
+        flat_b[d : d + 1] = recv_b[d]
 
     turned = jnp.transpose(flat_b[...])[0:16]
     high, low = split(turned)
@@ -721,16 +746,16 @@
 
     for copy in pending:
         copy.wait_send()
-    wait_all(stage_a, n_azim, 0)
-    wait_all(recv_a, n_axial, 2)
-    wait_all(stage_b, n_axial, 4)
-    wait_all(recv_b, n_azim, 6)
+    wait_all(recv_a, 0)
+    wait_all(recv_b, 2)
 
 
 def on_device(
     residual, element_scale, basis_fine, eigen_fine, operator_fine, basis_mid, eigen_mid,
     operator_mid, basis_low, eigen_low, prolong_mid, prolong_low, vertex_route, coarse_inverse,
 ):
+    devices = lax.axis_size("axial") * lax.axis_size("azim")
+
     def vm(*shape, dtype=F32):
         return pltpu.VMEM(shape, dtype)
 
@@ -755,12 +780,14 @@
         vm(1, 2, 64, 256, dtype=BF), vm(1, 256, 48, dtype=BF),
         vm(1536, 3072), vm(64, 768, dtype=BF), vm(128, 768), vm(128, 768, dtype=BF),
         vm(16, 768), vm(128, 3072, dtype=BF), vm(8, 3072), vm(1536, 128),
-        vm(64, 128), vm(2, 32, 1, 128), vm(4, 32, 1, 128), vm(32, 4, 1, 128),
-        vm(128, 128), vm(32, 4, 1, 128), vm(32, 4, 1, 128), vm(4, 32, 1, 128),
+        vm(64, 128), vm(64, 1, 128), vm(devices, 1, 128),
+        vm(devices, 128), vm(devices, 1, 128), vm(devices, 1, 128),
         vm(24, 64), vm(2, 1, 64), vm(24, 64), vm(3, 1, 64),
+        vm(16, 256), vm(16, 128), vm(16, 64),
         *face_buffers(4, *fine), *face_buffers(3, *mid), *face_buffers(2, *low),
         pltpu.SemaphoreType.DMA((10, 8)), pltpu.SemaphoreType.DMA((10, 8)),
-        pltpu.SemaphoreType.DMA((2,)), pltpu.SemaphoreType.DMA((8,)),
+        pltpu.SemaphoreType.DMA((2,)), pltpu.SemaphoreType.DMA((4,)),
+        pltpu.SemaphoreType.REGULAR,
     ]
     in_vmem = pl.BlockSpec(memory_space=pltpu.VMEM)
     in_smem = pl.BlockSpec(memory_space=pltpu.SMEM)

time: 89.7 us -> 84.5 us (0.942)
  Pallas kernels: 86.8 us -> 81.6 us
    pallas_call x1, Pallas kernels: 86.8 us -> 81.6 us  [on_device(): call(residual, jnp.transpose(element_scale, (0, 2, 1, 3)), vertex_route.r...]
where the time goes in v2:
time: 84.5 us; the launch traced here: 84.3 us
  Pallas kernels  81.6 us (97%)
  local copies, waits for them, and re-layouts  2.69 us (3%)
    pallas_call x1, Pallas kernels, on_device(): call(residual, jnp.transpose(element_scale, (0, 2, 1, 3)), vertex_route.r...  81.6 us
    unnamed x1, local copies, waits for them, and re-layouts  2.69 us

profile of v2, /device:TPU:1, one launch (start us, length us, event | category | flops | bytes accessed | tf_op | source)
XLA Modules:
  0.0 84.3 jit_solution(16670733511383806297)
XLA Ops:
  0.0 81.6 %shard_map.136 = f32[16,96,256]{2,1,0:T(8,128)} custom-call(f32[16,96,256]{2,1,0:T(8,128)} %res_hbm.1, f32[3,12,2,32]{3,2,1,0:T(2,128)} %bitcast.4, s32[1,768]{1,0:T(1,128)} %bitcast.5, f32[1,1,1536,3072]{3,2,1,0:T(8,128)} %inverse_hbm.1, f32[8,8]{1,0:T(8,128)} %bf_ref.1, f32[8]{0:T(128)} %ef_ref.1, f32[8,8]{1,0:T(8,128)} %qf_ref.1, f32[4,4]{1,0:T(4,128)} %bm_ref.1, ...), custom_call_target="tpu_custom_call" | custom-call | flops 12000000000 | bytes 24000000 | tf_op jit(solution)/shard_map/pallas_call | solution.py:810
  81.6 2.7 %copy.16 = f32[16,96,256]{2,1,0:T(8,128)} copy(f32[16,96,256]{2,1,0:T(8,128)} %shard_map.136) | data formatting | bytes 3145728

commit v3 on v2

--- a/solution.py
+++ b/solution.py
@@ -263,7 +263,7 @@
 def kernel(
     res_hbm, scale_ref, route_ref, inverse_hbm,
     bf_ref, ef_ref, qf_ref, bm_ref, em_ref, qm_ref, bl_ref, el_ref, pm_ref, plow_ref,
-    out_ref,
+    out_hbm,
     res, first, second, work, scale_f, inv_f, rhs_m, smooth_m, work_m, scale_m, inv_m,
     rhs_l, smooth_l, inv_l, total_l,
     right_f, left_f, right_rf, left_rf, right_pf, left_pf,
@@ -274,7 +274,7 @@
     fs_ax, fr_ax, fs_az, fr_az, fs_dg, fr_dg,
     ms_ax, mr_ax, ms_az, mr_az, ms_dg, mr_dg,
     ls_ax, lr_ax, ls_az, lr_az, ls_dg, lr_dg,
-    send_sem, recv_sem, load_sem, all_sem, word_sem,
+    send_sem, recv_sem, load_sem, all_sem, word_sem, out_sem,
     *, n_axial, n_azim,
 ):
     devices = n_axial * n_azim
@@ -336,48 +336,73 @@
             )
         return made
 
-    def send_faces(e, slot, n, buf, step, weighted):
+    def join_pairs(buf, planes, step):
+        if step is not None:
+            for at in range(step, buf.shape[1], step):
+                both = buf[planes, at - 1 : at, :] + buf[planes, at : at + 1, :]
+                buf[planes, at - 1 : at, :] = both
+                buf[planes, at : at + 1, :] = both
+
+    def send_ends(e, slot, n, buf, step):
         planes, rows, _ = buf.shape
-        if step is not None:
-            for at in range(step, rows, step):
-                both = buf[:, at - 1 : at, :] + buf[:, at : at + 1, :]
-                buf[:, at - 1 : at, :] = both
-                buf[:, at : at + 1, :] = both
-        both = buf[n - 1] + buf[n]
-        if weighted:
-            both = 0.5 * both
-        buf[n - 1] = both
-        buf[n] = both
-        s_ax, _, s_az, _, s_dg, _ = faces[n]
+        join_pairs(buf, slice(0, 1), step)
+        join_pairs(buf, slice(planes - 1, planes), step)
+        s_ax, s_dg = faces[n][0], faces[n][4]
         s_ax[slot, 0] = buf[planes - 1]
         s_ax[slot, 1] = buf[0]
         s_dg[slot, 0] = buf[planes - 1, rows - 1 : rows]
         s_dg[slot, 1] = buf[planes - 1, 0:1]
         s_dg[slot, 2] = buf[0, rows - 1 : rows]
         s_dg[slot, 3] = buf[0, 0:1]
+        made = copies_of(e, slot, n)
+        for copy in made[4:] + made[:2]:
+            copy.start()
+        pending.extend(made)
+        return made
+
+    def send_rows(made, slot, n, buf, step, weighted):
+        planes, rows, _ = buf.shape
+        join_pairs(buf, slice(1, planes - 1), step)
+        both = buf[n - 1] + buf[n]
+        if weighted:
+            both = 0.5 * both
+        buf[n - 1] = both
+        buf[n] = both
+        s_az = faces[n][2]
         for i in range(planes):
             s_az[slot, 0, i : i + 1] = buf[i, rows - 1 : rows]
             s_az[slot, 1, i : i + 1] = buf[i, 0:1]
-        made = copies_of(e, slot, n)
-        for copy in made[4:] + made[:4]:
+        for copy in made[2:4]:
             copy.start()
-        pending.extend(made)
+
+    def send_faces(e, slot, n, buf, step, weighted):
+        made = send_ends(e, slot, n, buf, step)
+        send_rows(made, slot, n, buf, step, weighted)
         return made
 
-    def join_faces(made, slot, n, buf, weighted):
+    def join_rows(made, slot, n, buf):
         planes, rows, _ = buf.shape
-        _, r_ax, _, r_az, _, _ = faces[n]
-        for copy in made[:4]:
+        r_az = faces[n][3]
+        for copy in made[2:4]:
             copy.wait_recv()
         for i in range(planes):
             buf[i, 0:1] = buf[i, 0:1] + r_az[slot, 0, i : i + 1]
             buf[i, rows - 1 : rows] = buf[i, rows - 1 : rows] + r_az[slot, 1, i : i + 1]
+
+    def join_planes(made, slot, n, buf, weighted):
+        planes, r_ax = buf.shape[0], faces[n][1]
+        for copy in made[:2]:
+            copy.wait_recv()
         for end, plane, device, weight in (
             (0, 0, first_device, weight_low_end),
             (1, planes - 1, last_device, weight_high_end),
         ):
             total = buf[plane] + jnp.where(device, 0.0, r_ax[slot, end])
             buf[plane] = total * weight if weighted else total
+
+    def join_faces(made, slot, n, buf, weighted):
+        join_rows(made, slot, n, buf)
+        join_planes(made, slot, n, buf, weighted)
 
     def join_corners(made, slot, n, buf, weighted):
         r_dg, hold = faces[n][5], holds[n]
@@ -427,14 +452,29 @@
         table = left_f[which]
         return wide_left(table, blocks[:half]) + wide_left(table, blocks[half:])
 
-    def fine_pass(x, which, factor, result, corners=None):
-        z = fine_left(fine_right(x, 2 * which, False), 2 * which)
+    def fine_pass(source, which, factor, result, e, weighted, came=None, corners=None):
+        if came is not None:
+            join_rows(*came[:4])
+        inner = fine_right(source(1, 15), 2 * which, False)
+        if came is not None:
+            join_planes(*came)
+        ends = jnp.concatenate([source(0, 1), source(15, 16)], 0)
+        ends = fine_right(ends, 2 * which, False)
+        z = fine_left(jnp.concatenate([ends[0:1], inner, ends[1:2]], 0), 2 * which)
         if corners is not None:
             lines = fine_right(corners().reshape(1, 16, 256), 2 * which, False).reshape(16, 256)
             z = add_corners(z, left_f[2 * which], FINE_CORNERS, lines)
         z = paste_rows(z, 8) * factor[...]
-        z = fine_right(z, 2 * which + 1, True)
-        result[...] = paste_rows(fine_left(z, 2 * which + 1), 8)
+        z = paste_rows(fine_left(z, 2 * which + 1), 8)
+        ends = fine_right(jnp.concatenate([z[0:1], z[15:16]], 0), 2 * which + 1, True)
+        result[0] = ends[0]
+        result[15] = ends[1]
+        if e == 0:
+            spread_word()
+        made = send_ends(e, e, 8, result, 16)
+        result[1:15] = fine_right(z[1:15], 2 * which + 1, True)
+        send_rows(made, e, 8, result, 16, weighted)
+        return made
 
     basis, basis_t = tables_of(bf_ref)
 
@@ -454,18 +494,15 @@
     put_scales(scale_ref, ef_ref, 8, scale_f, inv_f)
 
     load_res.wait()
-    fine_pass(res[...], 0, inv_f, first)
-    spread_word()
-    made = send_faces(0, 0, 8, first, 16, True)
+    made = fine_pass(lambda i, j: res[i:j], 0, inv_f, first, 0, True)
 
     oper, oper_t = tables_of(qf_ref)
     put_fine(1, oper, oper_t, False)
 
-    join_faces(made, 0, 8, first, True)
-    fine_pass(
-        first[...], 1, scale_f, work, lambda: join_corners(made, 0, 8, first, True)
+    came = (made, 0, 8, first, True)
+    made = fine_pass(
+        lambda i, j: first[i:j], 1, scale_f, work, 1, False, came, lambda: join_corners(*came)
     )
-    made = send_faces(1, 1, 8, work, 16, False)
 
     put_scales(scale_ref, em_ref, 4, scale_m, inv_m)
     pm, pm_t = tables_of(pm_ref, True)
@@ -481,25 +518,26 @@
         value = left_table(table, 4, 4, 4, joined=True, weighted=weighted, copies=2)
         put_left_twice(left_m, 2 * at + 1, value)
 
-    basis, basis_t = tables_of(bm_ref)
-    put_mid(0, basis, basis_t, True)
-
-    join_faces(made, 1, 8, work, False)
-    fine_pass(
-        res[...] - work[...], 0, inv_f, second, lambda: -join_corners(made, 1, 8, work, False)
+    came_work = (made, 1, 8, work, False)
+    made = fine_pass(
+        lambda i, j: res[i:j] - work[i:j], 0, inv_f, second, 2, True,
+        came_work, lambda: -join_corners(*came_work),
     )
-    made = send_faces(2, 2, 8, second, 16, True)
 
     oper, oper_t = tables_of(qm_ref)
     put_mid(1, oper, oper_t, False)
     put_scales(scale_ref, el_ref, 2, None, inv_l)
 
-    join_faces(made, 2, 8, second, True)
-    first[...] = first[...] + second[...]
-    fine_pass(
-        first[...], 1, scale_f, work, lambda: join_corners(made, 2, 8, first, True)
+    came_second = (made, 2, 8, second, True)
+
+    def joined_first():
+        first[...] = first[...] + second[...]
+        return join_corners(made, 2, 8, first, True)
+
+    made = fine_pass(
+        lambda i, j: first[i:j] + second[i:j], 1, scale_f, work, 3, False,
+        came_second, joined_first,
     )
-    made = send_faces(3, 3, 8, work, 16, False)
 
     plow, plow_t = tables_of(plow_ref, True)
     value = right_table(plow, 2, 4, joined=True, weigh_input=True, copies=2)
@@ -541,12 +579,14 @@
     target_hot[...] = hot.astype(BF)
     earlier = picked(iota((768, 768), 0) < iota((768, 768), 1)).astype(BF)
     rank = jnp.sum(mm(target_hot[...], earlier) * hot, axis=0, keepdims=True)
-    slot_hot[...] = picked(iota((128, 768), 0).astype(F32) == rank)
+    slot_hot[...] = jnp.transpose(picked(iota((128, 768), 0).astype(F32) == rank)).astype(BF)
     half = jnp.where(rank >= HALF_CAP, 1.0, 0.0)
     owner = 2 * route + jnp.where(rank >= HALF_CAP, 1, 0)
     row_hot[...] = picked(iota((128, 768), 0) == owner).astype(BF)
     place_hot[...] = picked(iota((16, 768), 0).astype(F32) == rank - HALF_CAP * half)
 
+    basis, basis_t = tables_of(bm_ref)
+    put_mid(0, basis, basis_t, True)
     join_faces(made, 0, 4, rhs_m, False)
 
     def mid_right(x, at):
@@ -607,11 +647,8 @@
         wide = jnp.dot(rhs_l[2 * a], pick_r, precision=HIGHEST, preferred_element_type=F32)
         values.append(jnp.sum(jnp.where(mine, wide, 0.0), axis=0, keepdims=True))
     values = jnp.concatenate(values, 1)
-    high, low = split(slot_hot[...] * values)
-    nt = (((1,), (1,)), ((), ()))
-    flat_a[...] = lax.dot_general(
-        target_hot[...], high, nt, preferred_element_type=F32
-    ) + lax.dot_general(target_hot[...], low, nt, preferred_element_type=F32)
+    both = mm(jnp.concatenate(split(target_hot[...].astype(F32) * values), 0), slot_hot[...])
+    flat_a[...] = both[:64] + both[64:]
     for t in range(64):
         send_a[t] = flat_a[t : t + 1]
 
@@ -692,7 +729,7 @@
 
     x = wide_right(smooth_m[...].reshape(384, 128), right_pf[0]).reshape(8, 48, 256)
     x = paste_rows(thrice_left(left_pf[0], cut_rows(x, 4, 16)), 8)
-    out_ref[...] = first[...] + x
+    second[...] = first[...] + x
     join_faces(made, 1, 2, smooth_l, True)
     join_corners(made, 1, 2, smooth_l, True)
 
@@ -742,12 +779,23 @@
     total_l[3] = smooth_l[3] + beyond
 
     wide = mm_right(total_l[...].reshape(96, 64), right_pp.at[0]).reshape(4, 24, 256)
-    out_ref[...] += paste_rows(thrice_left(left_pp[0], cut_rows(wide, 2, 8)), 8)
+    out_copies = []
+    for a in range(2):
+        z = thrice_left(left_pp[0], cut_rows(wide[2 * a : 2 * a + 2], 2, 8))
+        z = jnp.concatenate([b.reshape(8, 32, 256) for b in z], 1)
+        part = pl.ds(8 * a, 8)
+        second[part] = second[part] + z
+        out_copies.append(
+            pltpu.make_async_copy(second.at[part], out_hbm.at[part], out_sem.at[a])
+        )
+        out_copies[a].start()
 
     for copy in pending:
         copy.wait_send()
     wait_all(recv_a, 0)
     wait_all(recv_b, 2)
+    for copy in out_copies:
+        copy.wait()
 
 
 def on_device(
@@ -778,7 +826,7 @@
         vm(1, 256, 128, dtype=BF), vm(1, 32, 128, dtype=BF),
         vm(2, 2, 64, 64, dtype=BF), vm(2, 2, 48, 48, dtype=BF),
         vm(1, 2, 64, 256, dtype=BF), vm(1, 256, 48, dtype=BF),
-        vm(1536, 3072), vm(64, 768, dtype=BF), vm(128, 768), vm(128, 768, dtype=BF),
+        vm(1536, 3072), vm(64, 768, dtype=BF), vm(768, 128, dtype=BF), vm(128, 768, dtype=BF),
         vm(16, 768), vm(128, 3072, dtype=BF), vm(8, 3072), vm(1536, 128),
         vm(64, 128), vm(64, 1, 128), vm(devices, 1, 128),
         vm(devices, 128), vm(devices, 1, 128), vm(devices, 1, 128),
@@ -787,7 +835,7 @@
         *face_buffers(4, *fine), *face_buffers(3, *mid), *face_buffers(2, *low),
         pltpu.SemaphoreType.DMA((10, 8)), pltpu.SemaphoreType.DMA((10, 8)),
         pltpu.SemaphoreType.DMA((2,)), pltpu.SemaphoreType.DMA((4,)),
-        pltpu.SemaphoreType.REGULAR,
+        pltpu.SemaphoreType.REGULAR, pltpu.SemaphoreType.DMA((2,)),
     ]
     in_vmem = pl.BlockSpec(memory_space=pltpu.VMEM)
     in_smem = pl.BlockSpec(memory_space=pltpu.SMEM)
@@ -798,7 +846,7 @@
         ),
         out_shape=jax.ShapeDtypeStruct(residual.shape, F32),
         in_specs=[anywhere, in_vmem, in_vmem, anywhere] + [in_smem] * 10,
-        out_specs=in_vmem,
+        out_specs=anywhere,
         scratch_shapes=scratch,
         compiler_params=pltpu.CompilerParams(
             collective_id=0, has_side_effects=True, vmem_limit_bytes=58 * 1024 * 1024

time: 84.5 us -> 82.4 us (0.975)
  Pallas kernels: 81.6 us -> 79.5 us
    pallas_call x1, Pallas kernels: 81.6 us -> 79.5 us  [on_device(): call(residual, jnp.transpose(element_scale, (0, 2, 1, 3)), vertex_route.r...]
where the time goes in v3:
time: 82.4 us; the launch traced here: 82.2 us
  Pallas kernels  79.5 us (96%)
  local copies, waits for them, and re-layouts  2.69 us (3%)
    pallas_call x1, Pallas kernels, on_device(): call(residual, jnp.transpose(element_scale, (0, 2, 1, 3)), vertex_route.r...  79.5 us
    unnamed x1, local copies, waits for them, and re-layouts  2.69 us

profile of v3, /device:TPU:1, one launch (start us, length us, event | category | flops | bytes accessed | tf_op | source)
XLA Modules:
  0.0 82.2 jit_solution(5256218706655452688)
XLA Ops:
  0.0 79.5 %shard_map.136 = f32[16,96,256]{2,1,0:T(8,128)} custom-call(f32[16,96,256]{2,1,0:T(8,128)} %res_hbm.1, f32[3,12,2,32]{3,2,1,0:T(2,128)} %bitcast.4, s32[1,768]{1,0:T(1,128)} %bitcast.5, f32[1,1,1536,3072]{3,2,1,0:T(8,128)} %inverse_hbm.1, f32[8,8]{1,0:T(8,128)} %bf_ref.1, f32[8]{0:T(128)} %ef_ref.1, f32[8,8]{1,0:T(8,128)} %qf_ref.1, f32[4,4]{1,0:T(4,128)} %bm_ref.1, ...), custom_call_target="tpu_custom_call" | custom-call | flops 12000000000 | bytes 24000000 | tf_op jit(solution)/shard_map/pallas_call | solution.py:858
  79.5 2.7 %copy.16 = f32[16,96,256]{2,1,0:T(8,128)} copy(f32[16,96,256]{2,1,0:T(8,128)} %shard_map.136) | data formatting | bytes 3145728

commit v4 on v3

--- a/solution.py
+++ b/solution.py
@@ -764,24 +764,28 @@
             send_sem=send_sem.at[9, k], recv_sem=recv_sem.at[9, k],
             device_id=neighbour(da, dz), device_id_type=MESH,
         )
-        copy.start()
         made.append(copy)
     pending.extend(made)
-    for copy in made:
-        copy.wait_recv()
+    for k in (2, 0, 1):
+        made[k].start()
     last_row = iota((24, 64), 0) == 23
-    lower = jnp.where(last_row, cr_row[0], grids[0])
-    upper = jnp.where(last_row, cr_row[1], grids[1])
-    beyond = jnp.where(last_device, 0.0, jnp.where(last_row, cr_row[2], cr_plane[...]))
-    total_l[0] = smooth_l[0] + lower
-    total_l[1] = smooth_l[1] + upper
-    total_l[2] = smooth_l[2] + upper
-    total_l[3] = smooth_l[3] + beyond
-
-    wide = mm_right(total_l[...].reshape(96, 64), right_pp.at[0]).reshape(4, 24, 256)
     out_copies = []
     for a in range(2):
-        z = thrice_left(left_pp[0], cut_rows(wide[2 * a : 2 * a + 2], 2, 8))
+        if a == 0:
+            made[1].wait_recv()
+            near = jnp.where(last_row, cr_row[0], grids[0])
+            far = jnp.where(last_row, cr_row[1], grids[1])
+        else:
+            made[0].wait_recv()
+            made[2].wait_recv()
+            near = far
+            beyond = jnp.where(last_row, cr_row[2], cr_plane[...])
+            far = jnp.where(last_device, 0.0, beyond)
+        total_l[2 * a] = smooth_l[2 * a] + near
+        total_l[2 * a + 1] = smooth_l[2 * a + 1] + far
+        low = total_l[2 * a : 2 * a + 2].reshape(48, 64)
+        wide = mm_right(low, right_pp.at[0]).reshape(2, 24, 256)
+        z = thrice_left(left_pp[0], cut_rows(wide, 2, 8))
         z = jnp.concatenate([b.reshape(8, 32, 256) for b in z], 1)
         part = pl.ds(8 * a, 8)
         second[part] = second[part] + z

time: 82.4 us -> 82.1 us (level)
  no operation moved by 1% of the time
where the time goes in v4:
time: 82.1 us; the launch traced here: 81.9 us
  Pallas kernels  79.2 us (96%)
  local copies, waits for them, and re-layouts  2.69 us (3%)
    pallas_call x1, Pallas kernels, on_device(): call(residual, jnp.transpose(element_scale, (0, 2, 1, 3)), vertex_route.r...  79.2 us
    unnamed x1, local copies, waits for them, and re-layouts  2.69 us

profile of v4, /device:TPU:1, one launch (start us, length us, event | category | flops | bytes accessed | tf_op | source)
XLA Modules:
  0.0 81.9 jit_solution(4216694204788208476)
XLA Ops:
  0.0 79.2 %shard_map.136 = f32[16,96,256]{2,1,0:T(8,128)} custom-call(f32[16,96,256]{2,1,0:T(8,128)} %res_hbm.1, f32[3,12,2,32]{3,2,1,0:T(2,128)} %bitcast.4, s32[1,768]{1,0:T(1,128)} %bitcast.5, f32[1,1,1536,3072]{3,2,1,0:T(8,128)} %inverse_hbm.1, f32[8,8]{1,0:T(8,128)} %bf_ref.1, f32[8]{0:T(128)} %ef_ref.1, f32[8,8]{1,0:T(8,128)} %qf_ref.1, f32[4,4]{1,0:T(4,128)} %bm_ref.1, ...), custom_call_target="tpu_custom_call" | custom-call | flops 12000000000 | bytes 24000000 | tf_op jit(solution)/shard_map/pallas_call | solution.py:862
  79.2 2.7 %copy.16 = f32[16,96,256]{2,1,0:T(8,128)} copy(f32[16,96,256]{2,1,0:T(8,128)} %shard_map.136) | data formatting | bytes 3145728
